TPU v7x, 128 devices: a whole 4x4x4 slice. The times are simulated.
128 devices in a mesh: row: 8 (over x, y_lo), col: 16 (over z, y_hi, core).
Axes of the slice: x: 4, y: 4 (y_hi: 2, y_lo: 2; y = y_hi * 2 + y_lo), z: 4, core: 2. Of those that a mesh axis runs over, the one named last changes fastest.
Arguments:
- halves: float32 [2, 4096, 16384], P(None, 'row', 'col'), may hold values from -6 to 6
- diag_rest: float32 [8192, 1024], P(('col', 'row')), may hold values from -6 to 6
- panel_vectors: float32 [16384, 256], P('col'), may hold values from -1 to 1
- tri_factor: float32 [256, 256], replicated, may hold values from -1 to 2, as said below
Outputs:
- updated_halves: float32 [2, 4096, 16384], P(None, 'row', 'col')
- updated_rest: float32 [8192, 1024], P(('col', 'row'))
- w_panel: float32 [16384, 256], P('col')
Inputs may be any that keep to these rules, and one draw needn't show every extreme that they name: `tri_factor`: upper triangular, diagonal between 1 and 2.
All inputs are finite; a program needn't handle non-finite values.
Results may differ from a plain program's by a relative error of at most 0.0003.
Values sent between devices are 32-bit elements; how exact they have to be, the bound alone decides.
A program may use at most 64 MiB of HBM per device.

v0:
```python
import jax
import jax.numpy as jnp
from jax import lax
from jax.sharding import PartitionSpec as P

precise = lax.Precision.HIGHEST


def broadcast(value, axis, source):
    kept = jnp.where(lax.axis_index(axis) == source, value, 0).astype(value.dtype)
    return lax.psum(kept, axis)


def matmul(left, right):
    return jnp.dot(left, right, precision=precise, preferred_element_type=jnp.float32)


def left_contract(left, right):
    return lax.dot_general(
        left, right, (((0,), (0,)), ((), ())), precision=precise, preferred_element_type=jnp.float32
    )


def right_contract(left, right):
    return lax.dot_general(
        left, right, (((1,), (1,)), ((), ())), precision=precise, preferred_element_type=jnp.float32
    )


def shards(halves, diag_rest, panel_vectors, tri_factor):
    row_count = lax.axis_size("row")
    row_index = lax.axis_index("row")
    col_index = lax.axis_index("col")
    half_size = halves.shape[1]
    tile_size = halves.shape[2]
    panel_width = panel_vectors.shape[1]
    rest_rows = diag_rest.shape[0]
    rest_start = half_size + row_index * rest_rows
    zero_block = jnp.zeros((tile_size, panel_width), jnp.float32)
    row_vecs = []
    for position in range(2):
        row_vecs.append(broadcast(panel_vectors, "col", row_index + row_count * position))
    layout = []
    row_parts = []
    col_part = zero_block
    for position in range(2):
        block_row = row_index + row_count * position
        is_lower = block_row >= col_index
        weight = jnp.where(block_row == col_index, 0.5, 1.0).astype(jnp.float32)
        offset = jnp.where(is_lower, 0, half_size).astype(jnp.int32)
        low_vec = jnp.where(is_lower, panel_vectors, row_vecs[position])
        high_vec = jnp.where(is_lower, row_vecs[position], panel_vectors)
        high_half = lax.dynamic_slice_in_dim(high_vec, offset, half_size, 0)
        first = matmul(halves[position], low_vec) * weight
        second = left_contract(halves[position], high_half) * weight
        padded = lax.dynamic_update_slice_in_dim(zero_block, first, offset, 0)
        row_parts.append(jnp.where(is_lower, padded, second))
        col_part = col_part + jnp.where(is_lower, second, padded)
        layout.append((block_row, is_lower, offset, low_vec, high_half))
    own_rest_vec = lax.dynamic_slice_in_dim(panel_vectors, rest_start, rest_rows, 0)
    rest_first = lax.dynamic_update_slice_in_dim(
        zero_block, matmul(diag_rest, panel_vectors), rest_start, 0
    )
    col_part = col_part + 0.5 * (rest_first + left_contract(diag_rest, own_rest_vec))
    row_totals = lax.psum(jnp.stack(row_parts), "col")
    extra = zero_block
    for position in range(2):
        block_row = row_index + row_count * position
        extra = extra + jnp.where(block_row == col_index, row_totals[position], 0.0)
    col_terms = col_part + extra
    av_block = lax.psum(col_terms, "row")
    inner = lax.psum(left_contract(panel_vectors, av_block), "col")
    middle = matmul(left_contract(tri_factor, inner), tri_factor)
    w_own = matmul(av_block, tri_factor) - 0.5 * matmul(panel_vectors, middle)
    row_ws = []
    for position in range(2):
        row_ws.append(broadcast(w_own, "col", row_index + row_count * position))
    updated = []
    for position in range(2):
        block_row, is_lower, offset, low_vec, high_half = layout[position]
        low_w = jnp.where(is_lower, w_own, row_ws[position])
        high_w = jnp.where(is_lower, row_ws[position], w_own)
        high_whalf = lax.dynamic_slice_in_dim(high_w, offset, half_size, 0)
        left = jnp.concatenate([high_half, high_whalf], 1)
        right = jnp.concatenate([low_w, low_vec], 1)
        updated.append(halves[position] - right_contract(left, right))
    own_rest_w = lax.dynamic_slice_in_dim(w_own, rest_start, rest_rows, 0)
    left_rest = jnp.concatenate([own_rest_vec, own_rest_w], 1)
    right_rest = jnp.concatenate([w_own, panel_vectors], 1)
    new_rest = diag_rest - right_contract(left_rest, right_rest)
    return (jnp.stack(updated), new_rest, w_own)


def solution(mesh):
    return jax.shard_map(
        shards,
        mesh=mesh,
        in_specs=(P(None, "row", "col"), P(("col", "row"), None), P("col", None), P()),
        out_specs=(P(None, "row", "col"), P(("col", "row"), None), P("col", None)),
        check_vma=False,
    )
```

profile of v0, /device:TPU:1, one launch (start us, length us, event | category | flops | bytes accessed | tf_op | source)
XLA Modules:
  0.0 716.1 jit_solution(4993959610792432966)
XLA Ops:
  7.2 0.0 copy-start
  7.2 0.0 all-reduce.16.cloned.1.call-start
  7.2 1.6 copy.7
  8.8 1.6 broadcast_select_fusion.3
  10.5 0.0 all-reduce.16.cloned.1.call-update
  10.5 0.0 all-reduce.8.cloned.1.call-start
  10.6 149.3 %all-reduce.16.cloned.1.call-done = (f32[1024,256]{0,1:T(8,128)}, f32[1024,256]{0,1:T(8,128)}) async-done(((f32[1024,256]{0,1:T(8,128)}, f32[1024,256]{0,1:T(8,128)}), (f32[1024,256]{0,1:T(8,128)}, f32[1024,256]{0,1:T(8,128)})) %all-reduce.16.cloned.1.call-update) | async-done | bytes 2097168 | tf_op jit(solution)/shard_map/psum | solution.py:11
  159.9 1.7 broadcast_select_fusion.6
  161.6 0.0 copy-done.18
  161.6 0.0 copy-start.7
  161.6 0.0 copy-start.5
  161.6 2.2 dynamic-slice_select_fusion.3
  163.8 0.0 copy-start.12
  163.8 0.0 copy-start.14
  163.8 1.9 fusion.35
  165.7 1.9 fusion.41
  167.7 0.0 copy-done.12
  167.7 0.0 copy-done.14
  167.7 0.0 copy-start.10
  167.7 0.1 broadcast_in_dim.13.clone.1
  167.8 0.0 copy-done.7
  167.8 1.9 fusion.50
  169.8 0.1 broadcast_in_dim.13.clone
  169.9 0.0 copy-done.5
  169.9 1.9 fusion.59
  171.9 0.4 select_bitcast_fusion
  172.3 1.5 pad_maximum_fusion.1
  173.7 0.0 all-reduce.8.cloned.1.call-update
  173.8 0.2 all-reduce.10.cloned.1.call-start
  174.0 0.1 constant_dynamic-slice_fusion.1
  174.1 1.9 fusion.80
  176.0 0.0 copy-start.11
  176.0 1.0 copy-done.11
  177.0 0.0 copy-done.3
  177.0 3.4 convolution_add_fusion
  180.4 1.8 add.59
  182.2 138.4 %all-reduce.8.cloned.1.call-done = f32[2,1024,256]{1,2,0:T(8,128)} async-done(((f32[2,1024,256]{1,2,0:T(8,128)}), f32[2,1024,256]{1,2,0:T(8,128)}) %all-reduce.8.cloned.1.call-update) | async-done | bytes 2097168 | tf_op jit(solution)/shard_map/psum | solution.py:65
  320.6 4.3 fusion.67
  324.9 0.0 all-reduce.10.cloned.1.call-update
  325.0 0.0 all-reduce.12.cloned.1.call-start
  325.0 74.0 %all-reduce.10.cloned.1.call-done = f32[1024,256]{0,1:T(8,128)} async-done(((f32[1024,256]{0,1:T(8,128)}), f32[1024,256]{0,1:T(8,128)}) %all-reduce.10.cloned.1.call-update) | async-done | bytes 1048592 | tf_op jit(solution)/shard_map/psum | solution.py:71
  399.0 3.0 convolution_bitcast_fusion
  402.0 0.0 all-reduce.12.cloned.1.call-update
  402.1 0.0 all-reduce.14.cloned.1.call-start
  402.1 0.0 copy-done
  402.1 0.0 copy-done.16
  402.1 2.1 fusion.81
  404.2 139.3 %all-reduce.12.cloned.1.call-done = f32[256,256]{0,1:T(8,128)} async-done(((f32[256,256]{0,1:T(8,128)}), f32[256,256]{0,1:T(8,128)}) %all-reduce.12.cloned.1.call-update) | async-done | bytes 262160 | tf_op jit(solution)/shard_map/psum | solution.py:72
  543.5 1.4 fusion.82
  544.9 0.6 fusion.83
  545.5 3.3 broadcast_select_fusion.1
  548.9 0.0 all-reduce.14.cloned.1.call-update
  548.9 1.3 copy.17
  550.2 0.1 constant_dynamic-slice_fusion
  550.3 2.1 fusion.62
  552.4 143.3 %all-reduce.14.cloned.1.call-done = (f32[1024,256]{0,1:T(8,128)}, f32[1024,256]{0,1:T(8,128)}) async-done(((f32[1024,256]{0,1:T(8,128)}, f32[1024,256]{0,1:T(8,128)}), (f32[1024,256]{0,1:T(8,128)}, f32[1024,256]{0,1:T(8,128)})) %all-reduce.14.cloned.1.call-update) | async-done | bytes 2097168 | tf_op jit(solution)/shard_map/psum | solution.py:11
  695.7 1.6 dynamic-slice_select_fusion.1
  697.3 0.3 copy-done.20
  697.5 0.3 broadcast_select_fusion.7
  697.8 1.9 copy-done.2
  699.8 0.3 copy-done.8
  700.1 3.5 fusion.21
  703.6 3.6 fusion.16
  707.2 2.3 pad_maximum_fusion
  (25 shorter events, 0.0 us)
Async XLA Ops:
  7.2 395.0 %copy-start = (f32[256,256]{1,0:T(8,128)S(1)}, f32[256,256]{1,0:T(8,128)}, u32[]{:S(2)}) copy-start(f32[256,256]{1,0:T(8,128)} %param.7) | copy-start | bytes 786436
  7.2 152.7 %all-reduce.16.cloned.1.call-start = ((), (), s32[]{:S(2)}) async-start(), calls=%async_computation.4 | async-start | bytes 4194304 | tf_op jit(solution)/shard_map/psum | solution.py:11
  10.5 310.2 %all-reduce.8.cloned.1.call-start = ((), (), s32[]{:S(2)}) async-start(), calls=%async_computation | async-start | bytes 4194304 | tf_op jit(solution)/shard_map/psum | solution.py:65
  159.9 1.7 copy-start.18
  159.9 3.9 copy-start.1
  161.6 6.2 copy-start.7
  161.6 8.3 %copy-start.5 = (f32[1024,256]{0,1:T(8,128)}, f32[1024,256]{0,1:T(8,128)S(1)}, u32[]{:S(2)}) copy-start(f32[1024,256]{0,1:T(8,128)S(1)} %get-tuple-element.19) | copy-start | bytes 3145732
  163.8 3.9 copy-start.12
  163.8 3.9 copy-start.14
  165.7 6.1 copy-start.9
  167.7 4.2 copy-start.10
  169.8 2.1 copy-start.4
  173.7 3.3 copy-start.3
  173.8 225.2 %all-reduce.10.cloned.1.call-start = ((), (), s32[]{:S(2)}) async-start(), calls=%async_computation.1 | async-start | bytes 2097152 | tf_op jit(solution)/shard_map/psum | solution.py:71
  176.0 1.0 copy-start.11
  325.0 218.5 %all-reduce.12.cloned.1.call-start = ((), (), s32[]{:S(2)}) async-start(), calls=%async_computation.2 | async-start | bytes 524288 | tf_op jit(solution)/shard_map/psum | solution.py:72
  399.0 3.1 copy-start.16
  402.1 293.6 %all-reduce.14.cloned.1.call-start = ((), (), s32[]{:S(2)}) async-start(), calls=%async_computation.3 | async-start | bytes 4194304 | tf_op jit(solution)/shard_map/psum | solution.py:11
  543.5 2.0 copy-start.17
  548.9 1.4 copy-start.21
  695.7 1.6 copy-start.19
  695.7 1.9 copy-start.20
  695.7 2.1 copy-start.15
  697.5 2.2 copy-start.2
  697.5 2.5 copy-start.8
  700.1 3.5 copy-start.6
  700.1 3.6 copy-start.13
Sparse Core Ops, SparseCore 0:
  11.1 148.7 all-reduce.15
  173.9 146.7 all-reduce.7
  325.1 73.8 all-reduce.9
  402.2 141.2 all-reduce.11
  549.0 146.6 all-reduce.13
where the time goes:
time: 717 us; the launch traced here: 716 us
  waiting for transfers between devices  644 us (90%)
  matrix products  32.7 us (5%)
  other arithmetic  15.8 us (2%)
  between operations  14.2 us (2%)
  local copies, waits for them, and re-layouts  8.62 us (1%)
    psum x2, waiting for transfers between devices, broadcast(): return lax.psum(kept, axis)  293 us
    psum x1, waiting for transfers between devices, shards(): inner = lax.psum(left_contract(panel_vectors, av_block), 'col')  139 us
    psum x1, waiting for transfers between devices, shards(): row_totals = lax.psum(jnp.stack(row_parts), 'col')  138 us
    psum x1, waiting for transfers between devices, shards(): av_block = lax.psum(col_terms, 'row')  74 us
  transfers between devices with their start and end apart: 5, of which 5 were waited for; matrix products, arithmetic and copies ran while one was open for 2% of the time, Pallas kernels for 0%

commit v1 on v0

v1 whole, which is shorter than its diff:
```python
import functools

import jax
import jax.numpy as jnp
from jax import lax
from jax.experimental import pallas as pl
from jax.experimental.pallas import tpu as pltpu
from jax.sharding import PartitionSpec as P

MESH = pl.DeviceIdType.MESH
NN = (((1,), (0,)), ((), ()))
TN = (((0,), (0,)), ((), ()))
NT = (((1,), (1,)), ((), ()))
TILE = 1024
HALF = 512
WIDTH = 256
UNIT = 256
PIECE = 128
REST = 64


def split(value):
    high = value.astype(jnp.bfloat16)
    low = (value - high.astype(jnp.float32)).astype(jnp.bfloat16)
    return high, low


def product(left, right, dims):
    def dot(a, b):
        return lax.dot_general(a, b, dims, preferred_element_type=jnp.float32)

    return dot(left[0], right[0]) + (dot(left[0], right[1]) + dot(left[1], right[0]))


def rows(start, size):
    return pl.ds(pl.multiple_of(start, 8), size)


def place():
    row, col = lax.axis_index("row"), lax.axis_index("col")
    return dict(row=row, col=col, x=row // 2, lo=row % 2, z=col // 4, hi=(col // 2) % 2, core=col % 2)


def at(x, lo, z, hi, core):
    return (x * 2 + lo, z * 4 + hi * 2 + core)


def moved(me, x=0, y=0, z=0, core=0):
    y_at = (me["hi"] * 2 + me["lo"] + y) % 4
    return at((me["x"] + x) % 4, y_at % 2, (me["z"] + z) % 4, y_at // 2, (me["core"] + core) % 2)


class Copies:
    def __init__(self, send_sems, recv_sems):
        self.send_sems, self.recv_sems, self.used, self.started = send_sems, recv_sems, 0, []

    def make(self, source, target, device):
        copy = pltpu.make_async_remote_copy(
            src_ref=source,
            dst_ref=target,
            send_sem=self.send_sems.at[self.used],
            recv_sem=self.recv_sems.at[self.used],
            device_id=device,
            device_id_type=MESH,
        )
        self.used += 1
        return copy

    def start(self, source, target, device):
        copy = self.make(source, target, device)
        copy.start()
        self.started.append(copy)
        return copy

    def finish(self):
        for copy in self.started:
            copy.wait_send()


def ring_scatter(copies, source, out, relay, index, shift, plus, minus):
    def part(step, half):
        return source.at[rows(((index + step + shift) % 4) * UNIT + half * PIECE, PIECE)]

    far_plus = copies.start(part(2, 0), relay.at[0], plus)
    far_minus = copies.start(part(2, 1), relay.at[1], minus)
    near_plus = copies.start(part(1, 1), relay.at[2], plus)
    near_minus = copies.start(part(3, 0), relay.at[3], minus)
    yield
    far_plus.wait_recv()
    relay[6] = relay[0] + part(1, 0)[...]
    sum_plus = copies.start(relay.at[6], relay.at[4], plus)
    far_minus.wait_recv()
    relay[7] = relay[1] + part(3, 1)[...]
    sum_minus = copies.start(relay.at[7], relay.at[5], minus)
    yield
    near_plus.wait_recv()
    near_minus.wait_recv()
    sum_plus.wait_recv()
    sum_minus.wait_recv()
    out[0:PIECE] = part(0, 0)[...] + (relay[4] + relay[3])
    out[PIECE:UNIT] = part(0, 1)[...] + (relay[2] + relay[5])


def ring_gather(copies, block, index, shift, plus, minus, sibling=None):
    def unit(step):
        return block.at[rows(((index + step + shift) % 4) * UNIT, UNIT)]

    def half(step, which):
        return block.at[rows(((index + step + shift) % 4) * UNIT + which * PIECE, PIECE)]

    shared = []

    def share(ref):
        if sibling is not None:
            shared.append(copies.start(ref, ref, sibling))

    to_plus = copies.start(unit(0), unit(0), plus)
    to_minus = copies.start(unit(0), unit(0), minus)
    share(unit(0))
    yield
    to_plus.wait_recv()
    on_plus = copies.start(half(3, 0), half(3, 0), plus)
    to_minus.wait_recv()
    on_minus = copies.start(half(1, 1), half(1, 1), minus)
    share(unit(3))
    share(unit(1))
    yield
    on_plus.wait_recv()
    share(half(2, 0))
    on_minus.wait_recv()
    share(half(2, 1))
    yield
    for copy in shared:
        copy.wait_recv()


def inner_sum(copies, me, partial, total, work):
    first, first_in, second, second_in, third, third_in, fourth_in, fifth, sixth = work
    sibling = moved(me, core=1)
    core, x, y = me["core"], me["x"], me["hi"] * 2 + me["lo"]
    copy = copies.start(partial.at[rows((1 - core) * 128, 128)], first_in, sibling)
    yield
    copy.wait_recv()
    first[...] = partial[rows(core * 128, 128), :] + first_in[...]
    sent = [
        copies.start(first.at[rows(((x + d) % 4) * 32, 32)], second_in.at[d - 1], moved(me, x=d)) for d in (1, 2, 3)
    ]
    yield
    for copy in sent:
        copy.wait_recv()
    second[...] = first[rows(x * 32, 32), :] + second_in[0] + second_in[1] + second_in[2]
    sent = [copies.start(second.at[rows(((y + d) % 4) * 8, 8)], third_in.at[d - 1], moved(me, y=d)) for d in (1, 2, 3)]
    yield
    for copy in sent:
        copy.wait_recv()
    third[...] = second[rows(y * 8, 8), :] + third_in[0] + third_in[1] + third_in[2]
    sent = [copies.start(third, fourth_in.at[d - 1], moved(me, z=d)) for d in (1, 2, 3)]
    yield
    for copy in sent:
        copy.wait_recv()
    mine = fifth.at[rows(y * 8, 8)]
    mine[...] = third[...] + fourth_in[0] + fourth_in[1] + fourth_in[2]
    sent = [copies.start(mine, mine, moved(me, y=d)) for d in (1, 2, 3)]
    yield
    for copy in sent:
        copy.wait_recv()
    mine = sixth.at[rows(x * 32, 32)]
    mine[...] = fifth[...]
    sent = [copies.start(mine, mine, moved(me, x=d)) for d in (1, 2, 3)]
    yield
    for copy in sent:
        copy.wait_recv()
    mine = total.at[rows(core * 128, 128)]
    mine[...] = sixth[...]
    copy = copies.start(mine, mine, sibling)
    yield
    copy.wait_recv()


def step_all(running):
    still = []
    for item in running:
        if next(item, "done") != "done":
            still.append(item)
    return still


def gather_kernel(
    halves_ref, rest_ref, vec_ref, av_col, av_row, vec_row, inner_ref,
    tiles, parts, vec_high, vec_low, partial, row_sum, sibling_in, row_relay, col_relay,
    row_unit, col_unit, pair_in, swap_out, swap_in,
    first, first_in, second, second_in, third, third_in, fourth_in, fifth, sixth,
    load_sem, send_sems, recv_sems,
):
    me = place()
    row, col, core = me["row"], me["col"], me["core"]
    x, lo, z, hi = me["x"], me["lo"], me["z"], me["hi"]
    sibling = moved(me, core=1)

    row_shift = (x - (x // 2 + 2 * core) + 4) % 4
    row_half = (lo + hi + x) % 2
    as_row = (((z + row_shift) % 4) * 2 + row_half, row + 8 * core)
    row_of = col % 8
    as_col = at(row_of // 2, row_of % 2, (x - row_of // 2 + z + 4) % 4, (lo + row_of + hi) % 2, col // 8)
    alone = jnp.logical_and(as_row[0] == row, as_row[1] == col)

    load = pltpu.make_async_copy(halves_ref, tiles, load_sem)
    load.start()

    barrier = pltpu.get_barrier_semaphore()
    near = [moved(me, x=d) for d in (1, 2, 3)] + [moved(me, y=d) for d in (1, 2, 3)]
    near += [moved(me, z=d) for d in (1, 2, 3)] + [sibling]
    for device in near:
        pl.semaphore_signal(barrier, inc=1, device_id=device, device_id_type=MESH)

    @pl.when(jnp.logical_not(alone))
    def _():
        for device in (as_row, as_col):
            pl.semaphore_signal(barrier, inc=1, device_id=device, device_id_type=MESH)

    pl.semaphore_wait(barrier, len(near) + jnp.where(alone, 0, 2).astype(jnp.int32))

    copies = Copies(send_sems, recv_sems)
    z_ring = (z, row_shift, moved(me, z=1), moved(me, z=3))
    x_ring = (x, 0, moved(me, x=1), moved(me, x=3))

    own_rows = rows(x * UNIT, UNIT)
    mine_row = rows(((z + row_shift) % 4) * UNIT, UNIT)
    vec_block = vec_row.at[core]
    unit_copy = copies.make(vec_ref.at[own_rows], row_unit, as_col)

    @pl.when(jnp.logical_not(alone))
    def _():
        unit_copy.start()

    @pl.when(alone)
    def _():
        row_unit[...] = vec_ref[own_rows, :]

    parts[...] = jnp.zeros_like(parts)
    partial[...] = jnp.zeros_like(partial)
    vec_high[0], vec_low[0] = split(vec_ref[...])

    @pl.when(jnp.logical_not(alone))
    def _():
        unit_copy.wait_recv()
        unit_copy.wait_send()

    vec_block[mine_row, :] = row_unit[...]
    running = [ring_gather(copies, vec_block, *z_ring, sibling)]
    while running:
        running = step_all(running)
    for position in range(2):
        vec_high[1 + position], vec_low[1 + position] = split(vec_row[position])
    load.wait()

    def tile_rows(at_step, carry):
        position, chunk = at_step // 2, at_step % 2
        block_row = row + 8 * position
        is_lower = block_row >= col
        weight = jnp.where(block_row == col, 0.5, 1.0).astype(jnp.float32)
        offset = jnp.where(is_lower, 0, HALF) + chunk * UNIT
        low_at = jnp.where(is_lower, 0, 1 + position)
        high_at = jnp.where(is_lower, 1 + position, 0)
        block = split(tiles[position, rows(chunk * UNIT, UNIT), :])
        high_rows = rows(offset, UNIT)
        upper = (vec_high[high_at, high_rows, :], vec_low[high_at, high_rows, :])
        along = product(block, (vec_high[low_at], vec_low[low_at]), NN) * weight
        parts[high_at, high_rows, :] += along
        partial[...] += product(upper, split(along), TN)
        parts[low_at] += product(block, upper, TN) * weight
        return carry

    lax.fori_loop(0, 4, tile_rows, 0)
    rest_rows = rows(HALF + row * REST, REST)
    block = split(rest_ref[...])
    upper = (vec_high[0, rest_rows, :], vec_low[0, rest_rows, :])
    along = product(block, (vec_high[0], vec_low[0]), NN) * 0.5
    parts[0, rest_rows, :] += along
    partial[...] += product(upper, split(along), TN)
    parts[0] += product(block, upper, TN) * 0.5

    inner = inner_sum(
        copies, me, partial, inner_ref, (first, first_in, second, second_in, third, third_in, fourth_in, fifth, sixth)
    )
    pair = copies.start(parts.at[2 - core], sibling_in, sibling)
    columns = ring_scatter(copies, parts.at[0], col_unit, col_relay, *x_ring)
    next(columns)
    next(inner)
    pair.wait_recv()
    row_sum[...] = parts[1 + core] + sibling_in[...]
    running = [ring_scatter(copies, row_sum, row_unit, row_relay, *z_ring), columns, inner]
    while len(running) > 1:
        running = step_all(running)

    keep_row, keep_col = rows(row_half * PIECE, PIECE), rows(lo * PIECE, PIECE)
    give_row, give_col = rows((1 - row_half) * PIECE, PIECE), rows((1 - lo) * PIECE, PIECE)
    row_partner = moved(me, y=2)
    col_partner = at(x, 1 - lo, z, hi, core)
    row_copy = copies.start(row_unit.at[give_row], pair_in.at[0], row_partner)
    col_copy = copies.start(col_unit.at[give_col], pair_in.at[1], col_partner)
    step_all(running)
    row_copy.wait_recv()
    swap_out[0] = row_unit[keep_row, :] + pair_in[0]
    col_copy.wait_recv()
    swap_out[1] = col_unit[keep_col, :] + pair_in[1]
    row_copy = copies.make(swap_out.at[0], swap_in.at[0], as_row)
    col_copy = copies.make(swap_out.at[1], swap_in.at[1], as_col)

    @pl.when(jnp.logical_not(alone))
    def _():
        row_copy.start()
        col_copy.start()

    @pl.when(alone)
    def _():
        swap_in[...] = swap_out[...]

    step_all(running)

    @pl.when(jnp.logical_not(alone))
    def _():
        row_copy.wait()
        col_copy.wait()

    row_piece = av_row.at[core, rows(((z + row_shift) % 4) * UNIT + row_half * PIECE, PIECE)]
    col_piece = av_col.at[rows(x * UNIT + lo * PIECE, PIECE)]
    row_piece[...] = swap_out[0] + swap_in[1]
    col_piece[...] = swap_out[1] + swap_in[0]
    row_copy = copies.start(row_piece, row_piece, row_partner)
    col_copy = copies.start(col_piece, col_piece, col_partner)
    step_all(running)
    row_copy.wait_recv()
    col_copy.wait_recv()
    running = [
        ring_gather(copies, av_row.at[core], *z_ring, sibling),
        ring_gather(copies, av_col, *x_ring),
    ] + running
    while running:
        running = step_all(running)
    copies.finish()


def update_kernel(
    halves_ref, rest_ref, vec_ref, vec_row, av_col, av_row, inner_ref, tri_ref,
    out_ref, out_rest, out_w, vec_high, vec_low, w_high, w_low,
):
    row, col = lax.axis_index("row"), lax.axis_index("col")
    position, chunk = pl.program_id(0), pl.program_id(1)

    @pl.when(jnp.logical_and(position == 0, chunk == 0))
    def _():
        inner = inner_ref[...]
        tri = split(tri_ref[...])
        inner = inner + inner.T
        middle = product(tri, split(inner), TN)
        middle = split(product(split(middle), tri, NN) * 0.5)

        def block(at_step, carry):
            which, part = at_step // 4, at_step % 4
            here = rows(part * UNIT, UNIT)
            behind = jnp.maximum(which - 1, 0)
            own = which == 0
            vec = jnp.where(own, vec_ref[here, :], vec_row[behind, here, :])
            av = jnp.where(own, av_col[here, :], av_row[behind, here, :])
            vec = split(vec)
            w = product(split(av), tri, NN) - product(vec, middle, NN)
            vec_high[which, here, :], vec_low[which, here, :] = vec
            w_high[which, here, :], w_low[which, here, :] = split(w)

            @pl.when(own)
            def _():
                out_w[here, :] = w

            return carry

        lax.fori_loop(0, 12, block, 0)
        rest_rows = rows(HALF + row * REST, REST)
        update = product(
            (vec_high[0, rest_rows, :], vec_low[0, rest_rows, :]), (w_high[0], w_low[0]), NT
        ) + product((w_high[0, rest_rows, :], w_low[0, rest_rows, :]), (vec_high[0], vec_low[0]), NT)
        out_rest[...] = rest_ref[...] - update

    is_lower = row + 8 * position >= col
    size = halves_ref.shape[1]
    high_rows = rows(jnp.where(is_lower, 0, HALF) + chunk * size, size)
    low_at = jnp.where(is_lower, 0, 1 + position)
    high_at = jnp.where(is_lower, 1 + position, 0)
    update = product(
        (vec_high[high_at, high_rows, :], vec_low[high_at, high_rows, :]), (w_high[low_at], w_low[low_at]), NT
    ) + product((w_high[high_at, high_rows, :], w_low[high_at, high_rows, :]), (vec_high[low_at], vec_low[low_at]), NT)
    out_ref[0] = halves_ref[0] - update


def shards(halves, diag_rest, panel_vectors, tri_factor):
    vmem = pl.BlockSpec(memory_space=pltpu.VMEM)
    whole = pl.BlockSpec(memory_space=pl.ANY)
    f32 = jnp.float32
    block = (TILE, WIDTH)

    def buffer(*shape):
        return pltpu.VMEM(shape, f32)

    av_col, av_row, vec_row, inner = pl.pallas_call(
        gather_kernel,
        out_shape=[
            jax.ShapeDtypeStruct(block, f32),
            jax.ShapeDtypeStruct((2,) + block, f32),
            jax.ShapeDtypeStruct((2,) + block, f32),
            jax.ShapeDtypeStruct((WIDTH, WIDTH), f32),
        ],
        in_specs=[whole, vmem, vmem],
        out_specs=[vmem] * 4,
        scratch_shapes=[
            buffer(2, HALF, TILE),
            buffer(3, TILE, WIDTH),
            pltpu.VMEM((3, TILE, WIDTH), jnp.bfloat16),
            pltpu.VMEM((3, TILE, WIDTH), jnp.bfloat16),
            buffer(WIDTH, WIDTH),
            buffer(TILE, WIDTH),
            buffer(TILE, WIDTH),
            buffer(8, PIECE, WIDTH),
            buffer(8, PIECE, WIDTH),
            buffer(UNIT, WIDTH),
            buffer(UNIT, WIDTH),
            buffer(2, PIECE, WIDTH),
            buffer(2, PIECE, WIDTH),
            buffer(2, PIECE, WIDTH),
            buffer(128, WIDTH),
            buffer(128, WIDTH),
            buffer(32, WIDTH),
            buffer(3, 32, WIDTH),
            buffer(8, WIDTH),
            buffer(3, 8, WIDTH),
            buffer(3, 8, WIDTH),
            buffer(32, WIDTH),
            buffer(128, WIDTH),
            pltpu.SemaphoreType.DMA,
            pltpu.SemaphoreType.DMA((64,)),
            pltpu.SemaphoreType.DMA((64,)),
        ],
        compiler_params=pltpu.CompilerParams(
            collective_id=0, has_side_effects=True, vmem_limit_bytes=50 * 2**20
        ),
        name="gather",
    )(halves, diag_rest, panel_vectors)

    size = 128
    steps = HALF // size
    tile_block = pl.BlockSpec((1, size, TILE), lambda i, j: (i, j, 0))

    def fixed(*shape):
        return pl.BlockSpec(shape, lambda i, j: (0,) * len(shape))

    return pl.pallas_call(
        update_kernel,
        grid=(2, steps),
        out_shape=[
            jax.ShapeDtypeStruct(halves.shape, f32),
            jax.ShapeDtypeStruct(diag_rest.shape, f32),
            jax.ShapeDtypeStruct(panel_vectors.shape, f32),
        ],
        in_specs=[
            tile_block,
            fixed(REST, TILE),
            fixed(*block),
            fixed(2, *block),
            fixed(*block),
            fixed(2, *block),
            fixed(WIDTH, WIDTH),
            fixed(WIDTH, WIDTH),
        ],
        out_specs=[tile_block, fixed(REST, TILE), fixed(*block)],
        scratch_shapes=[pltpu.VMEM((3, TILE, WIDTH), jnp.bfloat16)] * 4,
        compiler_params=pltpu.CompilerParams(vmem_limit_bytes=50 * 2**20),
        name="update",
    )(halves, diag_rest, panel_vectors, vec_row, av_col, av_row, inner, tri_factor)


def solution(mesh):
    return jax.shard_map(
        shards,
        mesh=mesh,
        in_specs=(P(None, "row", "col"), P(("col", "row"), None), P("col", None), P()),
        out_specs=(P(None, "row", "col"), P(("col", "row"), None), P("col", None)),
        check_vma=False,
    )
```

time: 717 us -> 120 us (0.17)
  waiting for transfers between devices: 644 us -> 0 us
  Pallas kernels: 0 us -> 116 us
  matrix products: 32.7 us -> 0 us
  other arithmetic: 15.8 us -> 0 us
  between operations: 14.2 us -> 0.66 us
    psum x5 -> x0, waiting for transfers between devices: 644 us -> none  [the longest x2 293 us: broadcast(): return lax.psum(kept, axis)]
    pallas_call x0 -> x2, Pallas kernels: none -> 116 us  [the longest x1 97 us: shards(): pl.pallas_call(gather_kernel, out_shape=[jax.ShapeDtypeStruct(block, f32)...]
    dot_general x14 -> x0, matrix products: 32.7 us -> none  [the longest x6 13.3 us: matmul(): jnp.dot(left, right, precision=precise, preferred_element_type=jnp.float32)]
    select_n x5 -> x0, other arithmetic: 7.29 us -> none  [the longest x1 2.18 us: shards(): high_vec = jnp.where(is_lower, row_vecs[position], panel_vectors)]
  transfers between devices with their start and end apart: 5 -> 0, of which waited for: 5 -> 0; matrix products, arithmetic and copies ran while one was open for 2% -> 0% of each run, Pallas kernels for 0% -> 0%
where the time goes in v1:
time: 120 us; the launch traced here: 119 us
  Pallas kernels  116 us (97%)
  local copies, waits for them, and re-layouts  2.17 us (2%)
    pallas_call x1, Pallas kernels, shards(): pl.pallas_call(gather_kernel, out_shape=[jax.ShapeDtypeStruct(block, f32)...  97 us
    pallas_call x1, Pallas kernels, shards(): pl.pallas_call(update_kernel, grid=(2, steps), out_shape=[jax.ShapeDtypeS...  19.2 us

profile of v1, /device:TPU:1, one launch (start us, length us, event | category | flops | bytes accessed | tf_op | source)
XLA Modules:
  0.0 119.0 jit_solution(762836925263054983)
XLA Ops:
  0.6 0.0 copy-start
  0.6 1.2 %copy-done = f32[1024,256]{1,0:T(8,128)S(1)} copy-done((f32[1024,256]{1,0:T(8,128)S(1)}, f32[1024,256]{1,0:T(8,128)}, u32[]{:S(2)}) %copy-start) | copy-done | bytes 1048600
  1.9 0.0 copy-start.1
  1.9 0.9 copy-done.1
  2.8 0.0 copy-start.2
  2.8 97.0 %gather.1 = (f32[1024,256]{1,0:T(8,128)S(1)}, f32[2,1024,256]{2,1,0:T(8,128)}, f32[2,1024,256]{2,1,0:T(8,128)}, f32[256,256]{1,0:T(8,128)S(1)}) custom-call(f32[2,512,1024]{2,1,0:T(8,128)} %halves_ref.3, f32[64,1024]{1,0:T(8,128)S(1)} %copy-done.1, f32[1024,256]{1,0:T(8,128)S(1)} %copy-done), custom_call_target="tpu_custom_call" | custom-call | tf_op jit(solution)/shard_map/gather/pallas_call | solution.py:404
  99.8 0.0 copy-done.2
  99.8 19.2 %update.1 = (f32[2,512,1024]{2,1,0:T(8,128)}, f32[64,1024]{1,0:T(8,128)}, f32[1024,256]{1,0:T(8,128)}) custom-call(f32[2,512,1024]{2,1,0:T(8,128)} %halves_ref.3, f32[64,1024]{1,0:T(8,128)S(1)} %copy-done.1, f32[1024,256]{1,0:T(8,128)S(1)} %copy-done, f32[2,1024,256]{2,1,0:T(8,128)} %get-tuple-element.7.vec_row, f32[1024,256]{1,0:T(8,128)S(1)} %get-tuple-element.8.av_col, ...), custom_call_target="tpu_custom_call" | custom-call | tf_op jit(solution)/shard_map/update/pallas_call | solution.py:455
Async XLA Ops:
  0.6 1.2 %copy-start = (f32[1024,256]{1,0:T(8,128)S(1)}, f32[1024,256]{1,0:T(8,128)}, u32[]{:S(2)}) copy-start(f32[1024,256]{1,0:T(8,128)} %vec_ref.3) | copy-start | bytes 3145732
  1.9 0.9 copy-start.1
  2.8 97.0 %copy-start.2 = (f32[256,256]{1,0:T(8,128)S(1)}, f32[256,256]{1,0:T(8,128)}, u32[]{:S(2)}) copy-start(f32[256,256]{1,0:T(8,128)} %tri_ref.1) | copy-start | bytes 786436

commit v2 on v1

--- a/solution.py
+++ b/solution.py
@@ -101,37 +101,178 @@
     out[PIECE:UNIT] = part(0, 1)[...] + (relay[2] + relay[5])
 
 
-def ring_gather(copies, block, index, shift, plus, minus, sibling=None):
-    def unit(step):
-        return block.at[rows(((index + step + shift) % 4) * UNIT, UNIT)]
-
-    def half(step, which):
+def ring_gather(copies, block, index, shift, plus, minus, kept, partner, sibling=None):
+    def piece(step, which):
         return block.at[rows(((index + step + shift) % 4) * UNIT + which * PIECE, PIECE)]
 
+    given = 1 - kept
     shared = []
 
     def share(ref):
         if sibling is not None:
             shared.append(copies.start(ref, ref, sibling))
 
-    to_plus = copies.start(unit(0), unit(0), plus)
-    to_minus = copies.start(unit(0), unit(0), minus)
-    share(unit(0))
-    yield
-    to_plus.wait_recv()
-    on_plus = copies.start(half(3, 0), half(3, 0), plus)
-    to_minus.wait_recv()
-    on_minus = copies.start(half(1, 1), half(1, 1), minus)
-    share(unit(3))
-    share(unit(1))
-    yield
-    on_plus.wait_recv()
-    share(half(2, 0))
-    on_minus.wait_recv()
-    share(half(2, 1))
+    def send(ref, device):
+        return copies.start(ref, ref, device)
+
+    own = piece(0, kept)
+    pair = send(own, partner)
+    own_plus, own_minus = send(own, plus), send(own, minus)
+    share(own)
+    yield
+    pair.wait_recv()
+    other = piece(0, given)
+    other_plus, other_minus = send(other, plus), send(other, minus)
+    share(other)
+    yield
+    own_plus.wait_recv()
+    far_plus = send(piece(3, kept), plus)
+    share(piece(3, kept))
+    own_minus.wait_recv()
+    share(piece(1, kept))
+    yield
+    other_minus.wait_recv()
+    far_minus = send(piece(1, given), minus)
+    share(piece(1, given))
+    other_plus.wait_recv()
+    share(piece(3, given))
+    yield
+    far_plus.wait_recv()
+    share(piece(2, kept))
+    far_minus.wait_recv()
+    share(piece(2, given))
     yield
     for copy in shared:
         copy.wait_recv()
+
+
+ORDER = (0, 4, 1, 5, 2, 6, 3, 7)
+
+
+class Spread:
+    def __init__(self, me, vec_ref, vec_row, send_sems, recv_sems):
+        x, lo, z, hi, core = me["x"], me["lo"], me["z"], me["hi"], me["core"]
+        self.vec_ref, self.vec_row, self.send_sems, self.recv_sems = vec_ref, vec_row, send_sems, recv_sems
+        self.lead = core == lo
+        line = hi == x % 2
+        end = z % 2 == x // 2
+        self.source = jnp.logical_and(jnp.logical_and(self.lead, line), end)
+        self.cross = jnp.logical_and(jnp.logical_and(jnp.logical_not(self.lead), line), end)
+        self.target = jnp.logical_and(jnp.logical_and(self.lead, jnp.logical_not(line)), end)
+        self.ends = jnp.logical_and(self.lead, end)
+        self.middle = jnp.logical_and(self.lead, jnp.logical_not(end))
+        self.follow = jnp.logical_not(self.lead)
+        self.plus, self.minus, self.sibling = moved(me, z=1), moved(me, z=3), moved(me, core=1)
+        self.over = at(x, core, z, 1 - hi, core)
+        self.own = z // 2
+        self.from_minus = ((z + 3) % 4) // 2
+
+    def chunk(self, block, c):
+        return self.vec_row.at[block, pl.ds(c * PIECE, PIECE)]
+
+    def copy(self, slot, source, target, device):
+        return pltpu.make_async_remote_copy(
+            src_ref=source,
+            dst_ref=target,
+            send_sem=self.send_sems.at[slot],
+            recv_sem=self.recv_sems.at[slot],
+            device_id=device,
+            device_id_type=MESH,
+        )
+
+    def mine(self, c):
+        return self.vec_ref.at[pl.ds(c * PIECE, PIECE)]
+
+    def along(self, c, block, source=None):
+        here = self.chunk(block, c)
+        return self.copy(c, here if source is None else source, here, self.plus)
+
+    def back(self, c, block, source=None):
+        here = self.chunk(block, c)
+        return self.copy(8 + c, here if source is None else source, here, self.minus)
+
+    def across(self, c):
+        return self.copy(16 + c, self.mine(c), self.chunk(self.own, c), self.over)
+
+    def share(self, c, block, which, source=None):
+        here = self.chunk(block, c)
+        return self.copy(24 + 8 * which + c, here if source is None else source, here, self.sibling)
+
+    def begin(self):
+        @pl.when(self.source)
+        def _():
+            for c in ORDER:
+                self.along(c, self.own, self.mine(c)).start()
+                self.back(c, self.own, self.mine(c)).start()
+                self.share(c, self.own, 0, self.mine(c)).start()
+            self.vec_row[self.own] = self.vec_ref[...]
+
+        @pl.when(self.cross)
+        def _():
+            for c in ORDER:
+                self.across(c).start()
+
+    def serve(self, step):
+        c = ORDER[step]
+
+        @pl.when(self.target)
+        def _():
+            self.across(c).wait_recv()
+            self.along(c, self.own).start()
+            self.back(c, self.own).start()
+            self.share(c, self.own, 0).start()
+
+        @pl.when(self.middle)
+        def _():
+            block = self.from_minus
+            self.along(c, block).wait_recv()
+            if c < 4:
+                self.along(c, block).start()
+            self.share(c, block, 0).start()
+            self.back(c, 1 - block).wait_recv()
+            if c >= 4:
+                self.back(c, 1 - block).start()
+            self.share(c, 1 - block, 1).start()
+
+    def end(self):
+        @pl.when(self.ends)
+        def _():
+            for c in ORDER:
+                copy = self.along(c, 1 - self.own) if c < 4 else self.back(c, 1 - self.own)
+                copy.wait_recv()
+                self.share(c, 1 - self.own, 1).start()
+
+        @pl.when(self.follow)
+        def _():
+            for c in ORDER:
+                for which in range(2):
+                    self.share(c, which, which).wait_recv()
+
+    def finish(self):
+        @pl.when(self.ends)
+        def _():
+            for c in ORDER:
+                self.along(c, self.own).wait_send()
+                self.back(c, self.own).wait_send()
+
+        @pl.when(self.middle)
+        def _():
+            for c in ORDER:
+                if c < 4:
+                    self.along(c, 0).wait_send()
+                else:
+                    self.back(c, 0).wait_send()
+
+        @pl.when(self.lead)
+        def _():
+            for c in ORDER:
+                for which in range(2):
+                    self.share(c, which, which).wait_send()
+
+        @pl.when(self.cross)
+        def _():
+            for c in ORDER:
+                self.across(c).wait_send()
 
 
 def inner_sum(copies, me, partial, total, work):
@@ -187,10 +328,10 @@
 
 def gather_kernel(
     halves_ref, rest_ref, vec_ref, av_col, av_row, vec_row, inner_ref,
-    tiles, parts, vec_high, vec_low, partial, row_sum, sibling_in, row_relay, col_relay,
+    tiles, tile_high, tile_low, parts, rest_part, vec_high, vec_low, partial, row_sum, sibling_in, row_relay, col_relay,
     row_unit, col_unit, pair_in, swap_out, swap_in,
     first, first_in, second, second_in, third, third_in, fourth_in, fifth, sixth,
-    load_sem, send_sems, recv_sems,
+    load_sem, send_sems, recv_sems, vec_send_sems, vec_recv_sems,
 ):
     me = place()
     row, col, core = me["row"], me["col"], me["core"]
@@ -223,122 +364,141 @@
     copies = Copies(send_sems, recv_sems)
     z_ring = (z, row_shift, moved(me, z=1), moved(me, z=3))
     x_ring = (x, 0, moved(me, x=1), moved(me, x=3))
-
-    own_rows = rows(x * UNIT, UNIT)
-    mine_row = rows(((z + row_shift) % 4) * UNIT, UNIT)
-    vec_block = vec_row.at[core]
-    unit_copy = copies.make(vec_ref.at[own_rows], row_unit, as_col)
-
-    @pl.when(jnp.logical_not(alone))
-    def _():
-        unit_copy.start()
-
-    @pl.when(alone)
-    def _():
-        row_unit[...] = vec_ref[own_rows, :]
-
-    parts[...] = jnp.zeros_like(parts)
-    partial[...] = jnp.zeros_like(partial)
+    spread = Spread(me, vec_ref, vec_row, vec_send_sems, vec_recv_sems)
+    spread.begin()
     vec_high[0], vec_low[0] = split(vec_ref[...])
-
-    @pl.when(jnp.logical_not(alone))
-    def _():
-        unit_copy.wait_recv()
-        unit_copy.wait_send()
-
-    vec_block[mine_row, :] = row_unit[...]
-    running = [ring_gather(copies, vec_block, *z_ring, sibling)]
-    while running:
-        running = step_all(running)
+    load.wait()
+
+    def facts(position):
+        block_row = row + 8 * position
+        return block_row >= col, jnp.where(block_row == col, 0.5, 1.0).astype(jnp.float32)
+
+    def upper(which):
+        return vec_high[which, 0:HALF], vec_low[which, 0:HALF]
+
+    def lower(which):
+        return vec_high[which, HALF:TILE], vec_low[which, HALF:TILE]
+
+    def whole(which):
+        return vec_high[which], vec_low[which]
+
+    def row_part(position):
+        is_lower, weight = facts(position)
+        tile_high[position], tile_low[position] = split(tiles[position])
+        tile = tile_high.at[position], tile_low.at[position]
+
+        @pl.when(is_lower)
+        def _():
+            parts[1 + position, 0:HALF] = product((tile[0][...], tile[1][...]), whole(0), NN) * weight
+            parts[1 + position, HALF:TILE] = jnp.zeros((HALF, WIDTH), jnp.float32)
+
+        @pl.when(jnp.logical_not(is_lower))
+        def _():
+            parts[1 + position] = product((tile[0][...], tile[1][...]), lower(0), TN)
+
+    def col_part(position):
+        is_lower, weight = facts(position)
+        tile = tile_high.at[position], tile_low.at[position]
+
+        @pl.when(is_lower)
+        def _():
+            parts[0] += product((tile[0][...], tile[1][...]), upper(1 + position), TN) * weight
+
+        @pl.when(jnp.logical_not(is_lower))
+        def _():
+            parts[0, HALF:TILE] += product((tile[0][...], tile[1][...]), whole(1 + position), NN)
+
+    row_part(1 - core)
+    pair = copies.start(parts.at[2 - core], sibling_in, sibling)
+    spread.serve(0)
+    row_part(core)
+    spread.serve(1)
+    spread.serve(2)
+    rest_rows = rows(HALF + row * REST, REST)
+    block = split(rest_ref[...])
+    rest_part[...] = product(block, whole(0), NN) * 0.5
+    parts[0] = product(block, (vec_high[0, rest_rows, :], vec_low[0, rest_rows, :]), TN) * 0.5
+    spread.serve(3)
+    spread.serve(4)
+    pair.wait_recv()
+    row_sum[...] = parts[1 + core] + sibling_in[...]
+    for step in (5, 6, 7):
+        spread.serve(step)
+    row_scatter = ring_scatter(copies, row_sum, row_unit, row_relay, *z_ring)
+    next(row_scatter)
+    spread.end()
     for position in range(2):
         vec_high[1 + position], vec_low[1 + position] = split(vec_row[position])
-    load.wait()
-
-    def tile_rows(at_step, carry):
-        position, chunk = at_step // 2, at_step % 2
-        block_row = row + 8 * position
-        is_lower = block_row >= col
-        weight = jnp.where(block_row == col, 0.5, 1.0).astype(jnp.float32)
-        offset = jnp.where(is_lower, 0, HALF) + chunk * UNIT
-        low_at = jnp.where(is_lower, 0, 1 + position)
-        high_at = jnp.where(is_lower, 1 + position, 0)
-        block = split(tiles[position, rows(chunk * UNIT, UNIT), :])
-        high_rows = rows(offset, UNIT)
-        upper = (vec_high[high_at, high_rows, :], vec_low[high_at, high_rows, :])
-        along = product(block, (vec_high[low_at], vec_low[low_at]), NN) * weight
-        parts[high_at, high_rows, :] += along
-        partial[...] += product(upper, split(along), TN)
-        parts[low_at] += product(block, upper, TN) * weight
-        return carry
-
-    lax.fori_loop(0, 4, tile_rows, 0)
-    rest_rows = rows(HALF + row * REST, REST)
-    block = split(rest_ref[...])
-    upper = (vec_high[0, rest_rows, :], vec_low[0, rest_rows, :])
-    along = product(block, (vec_high[0], vec_low[0]), NN) * 0.5
-    parts[0, rest_rows, :] += along
-    partial[...] += product(upper, split(along), TN)
-    parts[0] += product(block, upper, TN) * 0.5
-
+    col_part(0)
+    next(row_scatter)
+    col_part(1)
+    partial[...] = product(whole(0), split(parts[0]), TN)
+    parts[0, rest_rows, :] += rest_part[...]
+    columns = ring_scatter(copies, parts.at[0], col_unit, col_relay, *x_ring)
+    next(columns)
     inner = inner_sum(
         copies, me, partial, inner_ref, (first, first_in, second, second_in, third, third_in, fourth_in, fifth, sixth)
     )
-    pair = copies.start(parts.at[2 - core], sibling_in, sibling)
-    columns = ring_scatter(copies, parts.at[0], col_unit, col_relay, *x_ring)
-    next(columns)
     next(inner)
-    pair.wait_recv()
-    row_sum[...] = parts[1 + core] + sibling_in[...]
-    running = [ring_scatter(copies, row_sum, row_unit, row_relay, *z_ring), columns, inner]
-    while len(running) > 1:
-        running = step_all(running)
+    step_all([row_scatter])
 
     keep_row, keep_col = rows(row_half * PIECE, PIECE), rows(lo * PIECE, PIECE)
     give_row, give_col = rows((1 - row_half) * PIECE, PIECE), rows((1 - lo) * PIECE, PIECE)
     row_partner = moved(me, y=2)
     col_partner = at(x, 1 - lo, z, hi, core)
     row_copy = copies.start(row_unit.at[give_row], pair_in.at[0], row_partner)
+    next(inner)
+    next(columns)
+    row_copy.wait_recv()
+    swap_out[...] = row_unit[keep_row, :] + pair_in[0]
+    row_copy = copies.make(swap_out, swap_in, as_row)
+
+    @pl.when(jnp.logical_not(alone))
+    def _():
+        row_copy.start()
+
+    @pl.when(alone)
+    def _():
+        swap_in[...] = swap_out[...]
+
+    next(inner)
+    step_all([columns])
     col_copy = copies.start(col_unit.at[give_col], pair_in.at[1], col_partner)
-    step_all(running)
-    row_copy.wait_recv()
-    swap_out[0] = row_unit[keep_row, :] + pair_in[0]
+    next(inner)
     col_copy.wait_recv()
-    swap_out[1] = col_unit[keep_col, :] + pair_in[1]
-    row_copy = copies.make(swap_out.at[0], swap_in.at[0], as_row)
-    col_copy = copies.make(swap_out.at[1], swap_in.at[1], as_col)
 
     @pl.when(jnp.logical_not(alone))
     def _():
+        row_copy.wait()
+
+    col_rows = rows(x * UNIT + lo * PIECE, PIECE)
+    col_piece = av_col.at[col_rows]
+    col_piece[...] = col_unit[keep_col, :] + pair_in[1] + swap_in[...]
+    row_copy = copies.make(col_piece, av_row.at[col // 8, col_rows], as_col)
+
+    @pl.when(jnp.logical_not(alone))
+    def _():
         row_copy.start()
-        col_copy.start()
 
     @pl.when(alone)
     def _():
-        swap_in[...] = swap_out[...]
-
-    step_all(running)
+        av_row[col // 8, col_rows, :] = col_piece[...]
+
+    columns = ring_gather(copies, av_col, *x_ring, lo, col_partner)
+    next(columns)
+    next(inner)
 
     @pl.when(jnp.logical_not(alone))
     def _():
         row_copy.wait()
-        col_copy.wait()
-
-    row_piece = av_row.at[core, rows(((z + row_shift) % 4) * UNIT + row_half * PIECE, PIECE)]
-    col_piece = av_col.at[rows(x * UNIT + lo * PIECE, PIECE)]
-    row_piece[...] = swap_out[0] + swap_in[1]
-    col_piece[...] = swap_out[1] + swap_in[0]
-    row_copy = copies.start(row_piece, row_piece, row_partner)
-    col_copy = copies.start(col_piece, col_piece, col_partner)
-    step_all(running)
-    row_copy.wait_recv()
-    col_copy.wait_recv()
-    running = [
-        ring_gather(copies, av_row.at[core], *z_ring, sibling),
-        ring_gather(copies, av_col, *x_ring),
-    ] + running
+
+    rows_in = ring_gather(copies, av_row.at[core], *z_ring, row_half, row_partner, sibling)
+    next(rows_in)
+    running = [columns, rows_in, inner]
     while running:
         running = step_all(running)
     copies.finish()
+    spread.finish()
 
 
 def update_kernel(
@@ -357,8 +517,8 @@
         middle = split(product(split(middle), tri, NN) * 0.5)
 
         def block(at_step, carry):
-            which, part = at_step // 4, at_step % 4
-            here = rows(part * UNIT, UNIT)
+            which, part = at_step // 2, at_step % 2
+            here = rows(part * HALF, HALF)
             behind = jnp.maximum(which - 1, 0)
             own = which == 0
             vec = jnp.where(own, vec_ref[here, :], vec_row[behind, here, :])
@@ -374,7 +534,7 @@
 
             return carry
 
-        lax.fori_loop(0, 12, block, 0)
+        lax.fori_loop(0, 6, block, 0)
         rest_rows = rows(HALF + row * REST, REST)
         update = product(
             (vec_high[0, rest_rows, :], vec_low[0, rest_rows, :]), (w_high[0], w_low[0]), NT
@@ -382,13 +542,19 @@
         out_rest[...] = rest_ref[...] - update
 
     is_lower = row + 8 * position >= col
-    size = halves_ref.shape[1]
-    high_rows = rows(jnp.where(is_lower, 0, HALF) + chunk * size, size)
+    size = halves_ref.shape[2]
+    high_rows, low_rows = rows(jnp.where(is_lower, 0, HALF), HALF), rows(chunk * size, size)
     low_at = jnp.where(is_lower, 0, 1 + position)
     high_at = jnp.where(is_lower, 1 + position, 0)
     update = product(
-        (vec_high[high_at, high_rows, :], vec_low[high_at, high_rows, :]), (w_high[low_at], w_low[low_at]), NT
-    ) + product((w_high[high_at, high_rows, :], w_low[high_at, high_rows, :]), (vec_high[low_at], vec_low[low_at]), NT)
+        (vec_high[high_at, high_rows, :], vec_low[high_at, high_rows, :]),
+        (w_high[low_at, low_rows, :], w_low[low_at, low_rows, :]),
+        NT,
+    ) + product(
+        (w_high[high_at, high_rows, :], w_low[high_at, high_rows, :]),
+        (vec_high[low_at, low_rows, :], vec_low[low_at, low_rows, :]),
+        NT,
+    )
     out_ref[0] = halves_ref[0] - update
 
 
@@ -413,7 +579,10 @@
         out_specs=[vmem] * 4,
         scratch_shapes=[
             buffer(2, HALF, TILE),
+            pltpu.VMEM((2, HALF, TILE), jnp.bfloat16),
+            pltpu.VMEM((2, HALF, TILE), jnp.bfloat16),
             buffer(3, TILE, WIDTH),
+            buffer(REST, WIDTH),
             pltpu.VMEM((3, TILE, WIDTH), jnp.bfloat16),
             pltpu.VMEM((3, TILE, WIDTH), jnp.bfloat16),
             buffer(WIDTH, WIDTH),
@@ -424,8 +593,8 @@
             buffer(UNIT, WIDTH),
             buffer(UNIT, WIDTH),
             buffer(2, PIECE, WIDTH),
-            buffer(2, PIECE, WIDTH),
-            buffer(2, PIECE, WIDTH),
+            buffer(PIECE, WIDTH),
+            buffer(PIECE, WIDTH),
             buffer(128, WIDTH),
             buffer(128, WIDTH),
             buffer(32, WIDTH),
@@ -436,8 +605,10 @@
             buffer(32, WIDTH),
             buffer(128, WIDTH),
             pltpu.SemaphoreType.DMA,
-            pltpu.SemaphoreType.DMA((64,)),
-            pltpu.SemaphoreType.DMA((64,)),
+            pltpu.SemaphoreType.DMA((80,)),
+            pltpu.SemaphoreType.DMA((80,)),
+            pltpu.SemaphoreType.DMA((40,)),
+            pltpu.SemaphoreType.DMA((40,)),
         ],
         compiler_params=pltpu.CompilerParams(
             collective_id=0, has_side_effects=True, vmem_limit_bytes=50 * 2**20
@@ -445,9 +616,9 @@
         name="gather",
     )(halves, diag_rest, panel_vectors)
 
-    size = 128
-    steps = HALF // size
-    tile_block = pl.BlockSpec((1, size, TILE), lambda i, j: (i, j, 0))
+    size = 256
+    steps = TILE // size
+    tile_block = pl.BlockSpec((1, HALF, size), lambda i, j: (i, 0, j))
 
     def fixed(*shape):
         return pl.BlockSpec(shape, lambda i, j: (0,) * len(shape))

time: 120 us -> 105 us (0.88)
  Pallas kernels: 116 us -> 101 us
    pallas_call x1, Pallas kernels: 97 us -> 85.8 us  [shards(): pl.pallas_call(gather_kernel, out_shape=[jax.ShapeDtypeStruct(block, f32)...]
    pallas_call x1, Pallas kernels: 19.2 us -> 15.6 us  [shards(): pl.pallas_call(update_kernel, grid=(2, steps), out_shape=[jax.ShapeDtypeS...]
where the time goes in v2:
time: 105 us; the launch traced here: 104 us
  Pallas kernels  101 us (96%)
  local copies, waits for them, and re-layouts  2.17 us (2%)
    pallas_call x1, Pallas kernels, shards(): pl.pallas_call(gather_kernel, out_shape=[jax.ShapeDtypeStruct(block, f32)...  85.8 us
    pallas_call x1, Pallas kernels, shards(): pl.pallas_call(update_kernel, grid=(2, steps), out_shape=[jax.ShapeDtypeS...  15.6 us
    unnamed x6, local copies, waits for them, and re-layouts  2.17 us

profile of v2, /device:TPU:1, one launch (start us, length us, event | category | flops | bytes accessed | tf_op | source)
XLA Modules:
  0.0 104.3 jit_solution(14161201266902107210)
XLA Ops:
  0.6 0.0 copy-start
  0.6 1.2 %copy-done = f32[1024,256]{1,0:T(8,128)S(1)} copy-done((f32[1024,256]{1,0:T(8,128)S(1)}, f32[1024,256]{1,0:T(8,128)}, u32[]{:S(2)}) %copy-start) | copy-done | bytes 1048600
  1.9 0.0 copy-start.1
  1.9 0.9 copy-done.1
  2.8 0.0 copy-start.2
  2.8 85.8 %gather.1 = (f32[1024,256]{1,0:T(8,128)S(1)}, f32[2,1024,256]{2,1,0:T(8,128)}, f32[2,1024,256]{2,1,0:T(8,128)}, f32[256,256]{1,0:T(8,128)S(1)}) custom-call(f32[2,512,1024]{2,1,0:T(8,128)} %halves_ref.3, f32[64,1024]{1,0:T(8,128)S(1)} %copy-done.1, f32[1024,256]{1,0:T(8,128)S(1)} %copy-done), custom_call_target="tpu_custom_call" | custom-call | tf_op jit(solution)/shard_map/gather/pallas_call | solution.py:570
  88.6 0.0 copy-done.2
  88.6 15.6 %update.1 = (f32[2,512,1024]{2,1,0:T(8,128)}, f32[64,1024]{1,0:T(8,128)}, f32[1024,256]{1,0:T(8,128)}) custom-call(f32[2,512,1024]{2,1,0:T(8,128)} %halves_ref.3, f32[64,1024]{1,0:T(8,128)S(1)} %copy-done.1, f32[1024,256]{1,0:T(8,128)S(1)} %copy-done, f32[2,1024,256]{2,1,0:T(8,128)} %get-tuple-element.7.vec_row, f32[1024,256]{1,0:T(8,128)S(1)} %get-tuple-element.8.av_col, ...), custom_call_target="tpu_custom_call" | custom-call | tf_op jit(solution)/shard_map/update/pallas_call | solution.py:626
Async XLA Ops:
  0.6 1.2 %copy-start = (f32[1024,256]{1,0:T(8,128)S(1)}, f32[1024,256]{1,0:T(8,128)}, u32[]{:S(2)}) copy-start(f32[1024,256]{1,0:T(8,128)} %vec_ref.3) | copy-start | bytes 3145732
  1.9 0.9 copy-start.1
  2.8 85.8 %copy-start.2 = (f32[256,256]{1,0:T(8,128)S(1)}, f32[256,256]{1,0:T(8,128)}, u32[]{:S(2)}) copy-start(f32[256,256]{1,0:T(8,128)} %tri_ref.1) | copy-start | bytes 786436

commit v3 on v2

--- a/solution.py
+++ b/solution.py
@@ -327,11 +327,12 @@
 
 
 def gather_kernel(
-    halves_ref, rest_ref, vec_ref, av_col, av_row, vec_row, inner_ref,
-    tiles, tile_high, tile_low, parts, rest_part, vec_high, vec_low, partial, row_sum, sibling_in, row_relay, col_relay,
+    halves_ref, rest_hbm, vec_hbm, tri_hbm, vec_high, vec_low, w_high, w_low, w_ref,
+    vec_ref, rest_ref, tri_ref, av_col, av_row, vec_row, inner_ref, vec_middle,
+    tiles, tile_high, tile_low, parts, rest_part, partial, row_sum, sibling_in, row_relay, col_relay,
     row_unit, col_unit, pair_in, swap_out, swap_in,
     first, first_in, second, second_in, third, third_in, fourth_in, fifth, sixth,
-    load_sem, send_sems, recv_sems, vec_send_sems, vec_recv_sems,
+    load_sems, send_sems, recv_sems, vec_send_sems, vec_recv_sems,
 ):
     me = place()
     row, col, core = me["row"], me["col"], me["core"]
@@ -345,8 +346,14 @@
     as_col = at(row_of // 2, row_of % 2, (x - row_of // 2 + z + 4) % 4, (lo + row_of + hi) % 2, col // 8)
     alone = jnp.logical_and(as_row[0] == row, as_row[1] == col)
 
-    load = pltpu.make_async_copy(halves_ref, tiles, load_sem)
-    load.start()
+    loads = [
+        pltpu.make_async_copy(source, target, load_sems.at[i])
+        for i, (source, target) in enumerate(
+            ((vec_hbm, vec_ref), (halves_ref, tiles), (rest_hbm, rest_ref), (tri_hbm, tri_ref))
+        )
+    ]
+    for load in loads:
+        load.start()
 
     barrier = pltpu.get_barrier_semaphore()
     near = [moved(me, x=d) for d in (1, 2, 3)] + [moved(me, y=d) for d in (1, 2, 3)]
@@ -365,9 +372,10 @@
     z_ring = (z, row_shift, moved(me, z=1), moved(me, z=3))
     x_ring = (x, 0, moved(me, x=1), moved(me, x=3))
     spread = Spread(me, vec_ref, vec_row, vec_send_sems, vec_recv_sems)
+    loads[0].wait()
     spread.begin()
     vec_high[0], vec_low[0] = split(vec_ref[...])
-    load.wait()
+    loads[1].wait()
 
     def facts(position):
         block_row = row + 8 * position
@@ -415,6 +423,7 @@
     spread.serve(1)
     spread.serve(2)
     rest_rows = rows(HALF + row * REST, REST)
+    loads[2].wait()
     block = split(rest_ref[...])
     rest_part[...] = product(block, whole(0), NN) * 0.5
     parts[0] = product(block, (vec_high[0, rest_rows, :], vec_low[0, rest_rows, :]), TN) * 0.5
@@ -471,9 +480,11 @@
     def _():
         row_copy.wait()
 
+    loads[3].wait()
+    tri = split(tri_ref[...])
     col_rows = rows(x * UNIT + lo * PIECE, PIECE)
     col_piece = av_col.at[col_rows]
-    col_piece[...] = col_unit[keep_col, :] + pair_in[1] + swap_in[...]
+    col_piece[...] = product(split(col_unit[keep_col, :] + pair_in[1] + swap_in[...]), tri, NN)
     row_copy = copies.make(col_piece, av_row.at[col // 8, col_rows], as_col)
 
     @pl.when(jnp.logical_not(alone))
@@ -487,6 +498,8 @@
     columns = ring_gather(copies, av_col, *x_ring, lo, col_partner)
     next(columns)
     next(inner)
+    next(columns)
+    next(inner)
 
     @pl.when(jnp.logical_not(alone))
     def _():
@@ -494,100 +507,123 @@
 
     rows_in = ring_gather(copies, av_row.at[core], *z_ring, row_half, row_partner, sibling)
     next(rows_in)
-    running = [columns, rows_in, inner]
-    while running:
-        running = step_all(running)
+    next(inner)
+    next(columns)
+    next(rows_in)
+    step_all([inner])
+    whole_inner = inner_ref[...] + inner_ref[...].T
+    middle = split(product(split(product(tri, split(whole_inner), TN)), tri, NN) * 0.5)
+    next(columns)
+    next(rows_in)
+    vec_middle[0] = product(whole(0), middle, NN)
+    next(columns)
+    next(rows_in)
+    vec_middle[1] = product(whole(1), middle, NN)
+    step_all([columns])
+    w = av_col[...] - vec_middle[0]
+    w_ref[...] = w
+    w_high[0], w_low[0] = split(w)
+    vec_middle[2] = product(whole(2), middle, NN)
+    next(rows_in)
+    step_all([rows_in])
+    for position in range(2):
+        w_high[1 + position], w_low[1 + position] = split(av_row[position] - vec_middle[1 + position])
     copies.finish()
     spread.finish()
 
 
 def update_kernel(
-    halves_ref, rest_ref, vec_ref, vec_row, av_col, av_row, inner_ref, tri_ref,
-    out_ref, out_rest, out_w, vec_high, vec_low, w_high, w_low,
+    halves_ref, rest_ref, vec_high, vec_low, w_high, w_low, w_ref, out_ref, out_rest, out_w,
+    tiles, rest, load_sems, store_sems, side_sems,
 ):
     row, col = lax.axis_index("row"), lax.axis_index("col")
-    position, chunk = pl.program_id(0), pl.program_id(1)
-
-    @pl.when(jnp.logical_and(position == 0, chunk == 0))
-    def _():
-        inner = inner_ref[...]
-        tri = split(tri_ref[...])
-        inner = inner + inner.T
-        middle = product(tri, split(inner), TN)
-        middle = split(product(split(middle), tri, NN) * 0.5)
-
-        def block(at_step, carry):
-            which, part = at_step // 2, at_step % 2
-            here = rows(part * HALF, HALF)
-            behind = jnp.maximum(which - 1, 0)
-            own = which == 0
-            vec = jnp.where(own, vec_ref[here, :], vec_row[behind, here, :])
-            av = jnp.where(own, av_col[here, :], av_row[behind, here, :])
-            vec = split(vec)
-            w = product(split(av), tri, NN) - product(vec, middle, NN)
-            vec_high[which, here, :], vec_low[which, here, :] = vec
-            w_high[which, here, :], w_low[which, here, :] = split(w)
-
-            @pl.when(own)
-            def _():
-                out_w[here, :] = w
-
-            return carry
-
-        lax.fori_loop(0, 6, block, 0)
-        rest_rows = rows(HALF + row * REST, REST)
+    count, _, size = tiles.shape
+    each = TILE // size
+
+    def place_of(ref, at_step):
+        return ref.at[at_step // each, :, pl.ds(pl.multiple_of((at_step % each) * size, size), size)]
+
+    def load(at_step):
+        return pltpu.make_async_copy(place_of(halves_ref, at_step), tiles.at[at_step], load_sems.at[at_step])
+
+    def store(at_step):
+        return pltpu.make_async_copy(tiles.at[at_step], place_of(out_ref, at_step), store_sems.at[at_step])
+
+    w_copy = pltpu.make_async_copy(w_ref, out_w, side_sems.at[0])
+    rest_in = pltpu.make_async_copy(rest_ref, rest, side_sems.at[1])
+    rest_out = pltpu.make_async_copy(rest, out_rest, side_sems.at[2])
+    for at_step in range(count):
+        load(at_step).start()
+    rest_in.start()
+    w_copy.start()
+
+    def one(at_step, carry):
+        position = at_step // each
+        is_lower = row + 8 * position >= col
+        high_rows = rows(jnp.where(is_lower, 0, HALF), HALF)
+        low_rows = rows((at_step % each) * size, size)
+        low_at = jnp.where(is_lower, 0, 1 + position)
+        high_at = jnp.where(is_lower, 1 + position, 0)
         update = product(
-            (vec_high[0, rest_rows, :], vec_low[0, rest_rows, :]), (w_high[0], w_low[0]), NT
-        ) + product((w_high[0, rest_rows, :], w_low[0, rest_rows, :]), (vec_high[0], vec_low[0]), NT)
-        out_rest[...] = rest_ref[...] - update
-
-    is_lower = row + 8 * position >= col
-    size = halves_ref.shape[2]
-    high_rows, low_rows = rows(jnp.where(is_lower, 0, HALF), HALF), rows(chunk * size, size)
-    low_at = jnp.where(is_lower, 0, 1 + position)
-    high_at = jnp.where(is_lower, 1 + position, 0)
+            (vec_high[high_at, high_rows, :], vec_low[high_at, high_rows, :]),
+            (w_high[low_at, low_rows, :], w_low[low_at, low_rows, :]),
+            NT,
+        ) + product(
+            (w_high[high_at, high_rows, :], w_low[high_at, high_rows, :]),
+            (vec_high[low_at, low_rows, :], vec_low[low_at, low_rows, :]),
+            NT,
+        )
+        load(at_step).wait()
+        tiles[at_step] = tiles[at_step] - update
+        store(at_step).start()
+        return carry
+
+    lax.fori_loop(0, count, one, 0)
+    rest_rows = rows(HALF + row * REST, REST)
     update = product(
-        (vec_high[high_at, high_rows, :], vec_low[high_at, high_rows, :]),
-        (w_high[low_at, low_rows, :], w_low[low_at, low_rows, :]),
-        NT,
-    ) + product(
-        (w_high[high_at, high_rows, :], w_low[high_at, high_rows, :]),
-        (vec_high[low_at, low_rows, :], vec_low[low_at, low_rows, :]),
-        NT,
-    )
-    out_ref[0] = halves_ref[0] - update
+        (vec_high[0, rest_rows, :], vec_low[0, rest_rows, :]), (w_high[0], w_low[0]), NT
+    ) + product((w_high[0, rest_rows, :], w_low[0, rest_rows, :]), (vec_high[0], vec_low[0]), NT)
+    rest_in.wait()
+    rest[...] = rest[...] - update
+    rest_out.start()
+    for at_step in range(count):
+        store(at_step).wait()
+    w_copy.wait()
+    rest_out.wait()
 
 
 def shards(halves, diag_rest, panel_vectors, tri_factor):
     vmem = pl.BlockSpec(memory_space=pltpu.VMEM)
-    whole = pl.BlockSpec(memory_space=pl.ANY)
+    outside = pl.BlockSpec(memory_space=pltpu.HBM)
     f32 = jnp.float32
     block = (TILE, WIDTH)
 
     def buffer(*shape):
         return pltpu.VMEM(shape, f32)
 
-    av_col, av_row, vec_row, inner = pl.pallas_call(
+    terms = jax.ShapeDtypeStruct((3,) + block, jnp.bfloat16)
+    handed = pl.pallas_call(
         gather_kernel,
-        out_shape=[
-            jax.ShapeDtypeStruct(block, f32),
-            jax.ShapeDtypeStruct((2,) + block, f32),
-            jax.ShapeDtypeStruct((2,) + block, f32),
-            jax.ShapeDtypeStruct((WIDTH, WIDTH), f32),
-        ],
-        in_specs=[whole, vmem, vmem],
-        out_specs=[vmem] * 4,
+        out_shape=[terms, terms, terms, terms, jax.ShapeDtypeStruct(block, f32)],
+        in_specs=[outside] * 4,
+        out_specs=[vmem] * 5,
         scratch_shapes=[
+            buffer(*block),
+            buffer(REST, TILE),
+            buffer(WIDTH, WIDTH),
+            buffer(*block),
+            buffer(2, *block),
+            buffer(2, *block),
+            buffer(WIDTH, WIDTH),
+            buffer(3, *block),
             buffer(2, HALF, TILE),
             pltpu.VMEM((2, HALF, TILE), jnp.bfloat16),
             pltpu.VMEM((2, HALF, TILE), jnp.bfloat16),
-            buffer(3, TILE, WIDTH),
+            buffer(3, *block),
             buffer(REST, WIDTH),
-            pltpu.VMEM((3, TILE, WIDTH), jnp.bfloat16),
-            pltpu.VMEM((3, TILE, WIDTH), jnp.bfloat16),
             buffer(WIDTH, WIDTH),
-            buffer(TILE, WIDTH),
-            buffer(TILE, WIDTH),
+            buffer(*block),
+            buffer(*block),
             buffer(8, PIECE, WIDTH),
             buffer(8, PIECE, WIDTH),
             buffer(UNIT, WIDTH),
@@ -604,48 +640,39 @@
             buffer(3, 8, WIDTH),
             buffer(32, WIDTH),
             buffer(128, WIDTH),
-            pltpu.SemaphoreType.DMA,
+            pltpu.SemaphoreType.DMA((4,)),
             pltpu.SemaphoreType.DMA((80,)),
             pltpu.SemaphoreType.DMA((80,)),
             pltpu.SemaphoreType.DMA((40,)),
             pltpu.SemaphoreType.DMA((40,)),
         ],
         compiler_params=pltpu.CompilerParams(
-            collective_id=0, has_side_effects=True, vmem_limit_bytes=50 * 2**20
+            collective_id=0, has_side_effects=True, vmem_limit_bytes=44 * 2**20
         ),
         name="gather",
-    )(halves, diag_rest, panel_vectors)
+    )(halves, diag_rest, panel_vectors, tri_factor)
 
     size = 256
-    steps = TILE // size
-    tile_block = pl.BlockSpec((1, HALF, size), lambda i, j: (i, 0, j))
-
-    def fixed(*shape):
-        return pl.BlockSpec(shape, lambda i, j: (0,) * len(shape))
-
+    count = 2 * TILE // size
     return pl.pallas_call(
         update_kernel,
-        grid=(2, steps),
         out_shape=[
             jax.ShapeDtypeStruct(halves.shape, f32),
             jax.ShapeDtypeStruct(diag_rest.shape, f32),
             jax.ShapeDtypeStruct(panel_vectors.shape, f32),
         ],
-        in_specs=[
-            tile_block,
-            fixed(REST, TILE),
-            fixed(*block),
-            fixed(2, *block),
-            fixed(*block),
-            fixed(2, *block),
-            fixed(WIDTH, WIDTH),
-            fixed(WIDTH, WIDTH),
+        in_specs=[outside] * 2 + [vmem] * 5,
+        out_specs=[outside] * 3,
+        scratch_shapes=[
+            buffer(count, HALF, size),
+            buffer(REST, TILE),
+            pltpu.SemaphoreType.DMA((count,)),
+            pltpu.SemaphoreType.DMA((count,)),
+            pltpu.SemaphoreType.DMA((3,)),
         ],
-        out_specs=[tile_block, fixed(REST, TILE), fixed(*block)],
-        scratch_shapes=[pltpu.VMEM((3, TILE, WIDTH), jnp.bfloat16)] * 4,
-        compiler_params=pltpu.CompilerParams(vmem_limit_bytes=50 * 2**20),
+        compiler_params=pltpu.CompilerParams(vmem_limit_bytes=24 * 2**20),
         name="update",
-    )(halves, diag_rest, panel_vectors, vec_row, av_col, av_row, inner, tri_factor)
+    )(halves, diag_rest, *handed)
 
 
 def solution(mesh):

time: 105 us -> 96.2 us (0.916)
  Pallas kernels: 101 us -> 91.7 us
  local copies, waits for them, and re-layouts: 2.17 us -> 3.5 us
    pallas_call x2, Pallas kernels: 101 us -> 91.7 us  [the longest x1 83.8 us: shards(): pl.pallas_call(gather_kernel, out_shape=[terms, terms, terms, terms, jax....]
    unnamed x6 -> x8, local copies, waits for them, and re-layouts: 2.17 us -> 3.5 us
where the time goes in v3:
time: 96.2 us; the launch traced here: 96 us
  Pallas kernels  91.7 us (95%)
  local copies, waits for them, and re-layouts  3.5 us (4%)
    pallas_call x1, Pallas kernels, shards(): pl.pallas_call(gather_kernel, out_shape=[terms, terms, terms, terms, jax....  83.8 us
    pallas_call x1, Pallas kernels, shards(): pl.pallas_call(update_kernel, out_shape=[jax.ShapeDtypeStruct(halves.shap...  7.88 us
    unnamed x8, local copies, waits for them, and re-layouts  3.5 us

profile of v3, /device:TPU:1, one launch (start us, length us, event | category | flops | bytes accessed | tf_op | source)
XLA Modules:
  0.0 96.0 jit_solution(5197210376141590116)
XLA Ops:
  0.6 0.0 copy-start
  0.6 0.0 copy-start.1
  0.7 1.1 %copy-done.1 = f32[64,1024]{1,0:T(8,128)S(1)} copy-done((f32[64,1024]{1,0:T(8,128)S(1)}, f32[64,1024]{1,0:T(8,128)}, u32[]{:S(2)}) %copy-start.1) | copy-done | bytes 262168
  1.7 0.0 copy-start.2
  1.7 1.5 %copy-done.2 = f32[1024,256]{1,0:T(8,128)S(1)} copy-done((f32[1024,256]{1,0:T(8,128)S(1)}, f32[1024,256]{1,0:T(8,128)}, u32[]{:S(2)}) %copy-start.2) | copy-done | bytes 1048600
  3.2 0.0 copy-start.3
  3.2 0.9 copy-done.3
  4.1 83.8 %gather.1 = (bf16[3,1024,256]{2,1,0:T(8,128)(2,1)S(1)}, bf16[3,1024,256]{2,1,0:T(8,128)(2,1)S(1)}, bf16[3,1024,256]{2,1,0:T(8,128)(2,1)S(1)}, bf16[3,1024,256]{2,1,0:T(8,128)(2,1)S(1)}, f32[1024,256]{1,0:T(8,128)S(1)}) custom-call(f32[2,512,1024]{2,1,0:T(8,128)} %halves_ref.3, f32[64,1024]{1,0:T(8,128)S(1)} %copy-done.1, f32[1024,256]{1,0:T(8,128)S(1)} %copy-done.2, ...), custom_call_target="tpu_custom_call" | custom-call | tf_op jit(solution)/shard_map/gather/pallas_call | solution.py:605
  88.0 0.0 copy-done
  88.0 7.9 %update.1 = (f32[2,512,1024]{2,1,0:T(8,128)}, f32[64,1024]{1,0:T(8,128)}, f32[1024,256]{1,0:T(8,128)}) custom-call(f32[2,512,1024]{2,1,0:T(8,128)S(1)} %copy-done, f32[64,1024]{1,0:T(8,128)S(1)} %copy-done.1, bf16[3,1024,256]{2,1,0:T(8,128)(2,1)S(1)} %get-tuple-element.8.vec_high, bf16[3,1024,256]{2,1,0:T(8,128)(2,1)S(1)} %get-tuple-element.9.vec_low, ...), custom_call_target="tpu_custom_call" | custom-call | tf_op jit(solution)/shard_map/update/pallas_call | solution.py:657
Async XLA Ops:
  0.6 87.3 %copy-start = (f32[2,512,1024]{2,1,0:T(8,128)S(1)}, f32[2,512,1024]{2,1,0:T(8,128)}, u32[]{:S(2)}) copy-start(f32[2,512,1024]{2,1,0:T(8,128)} %halves_ref.3) | copy-start | bytes 12582916
  0.6 1.1 %copy-start.1 = (f32[64,1024]{1,0:T(8,128)S(1)}, f32[64,1024]{1,0:T(8,128)}, u32[]{:S(2)}) copy-start(f32[64,1024]{1,0:T(8,128)} %rest_ref.1) | copy-start | bytes 786436
  1.7 1.5 %copy-start.2 = (f32[1024,256]{1,0:T(8,128)S(1)}, f32[1024,256]{1,0:T(8,128)}, u32[]{:S(2)}) copy-start(f32[1024,256]{1,0:T(8,128)} %vec_hbm.1) | copy-start | bytes 3145732
  3.2 0.9 copy-start.3

commit v4 on v3

--- a/solution.py
+++ b/solution.py
@@ -431,15 +431,15 @@
     spread.serve(4)
     pair.wait_recv()
     row_sum[...] = parts[1 + core] + sibling_in[...]
-    for step in (5, 6, 7):
-        spread.serve(step)
+    spread.serve(5)
     row_scatter = ring_scatter(copies, row_sum, row_unit, row_relay, *z_ring)
     next(row_scatter)
+    spread.serve(6)
+    spread.serve(7)
     spread.end()
-    for position in range(2):
-        vec_high[1 + position], vec_low[1 + position] = split(vec_row[position])
+    vec_high[1], vec_low[1] = split(vec_row[0])
     col_part(0)
-    next(row_scatter)
+    vec_high[2], vec_low[2] = split(vec_row[1])
     col_part(1)
     partial[...] = product(whole(0), split(parts[0]), TN)
     parts[0, rest_rows, :] += rest_part[...]
@@ -449,6 +449,11 @@
         copies, me, partial, inner_ref, (first, first_in, second, second_in, third, third_in, fourth_in, fifth, sixth)
     )
     next(inner)
+    loads[3].wait()
+    tri = split(tri_ref[...])
+    next(row_scatter)
+    next(inner)
+    next(columns)
     step_all([row_scatter])
 
     keep_row, keep_col = rows(row_half * PIECE, PIECE), rows(lo * PIECE, PIECE)
@@ -457,73 +462,65 @@
     col_partner = at(x, 1 - lo, z, hi, core)
     row_copy = copies.start(row_unit.at[give_row], pair_in.at[0], row_partner)
     next(inner)
-    next(columns)
+    step_all([columns])
+    col_copy = copies.start(col_unit.at[give_col], pair_in.at[1], col_partner)
     row_copy.wait_recv()
-    swap_out[...] = row_unit[keep_row, :] + pair_in[0]
-    row_copy = copies.make(swap_out, swap_in, as_row)
+    swap_out[0] = product(split(row_unit[keep_row, :] + pair_in[0]), tri, NN)
+    row_copy = copies.make(swap_out.at[0], swap_in.at[0], as_row)
 
     @pl.when(jnp.logical_not(alone))
     def _():
         row_copy.start()
 
+    next(inner)
+    col_copy.wait_recv()
+    swap_out[1] = product(split(col_unit[keep_col, :] + pair_in[1]), tri, NN)
+    col_copy = copies.make(swap_out.at[1], swap_in.at[1], as_col)
+
+    @pl.when(jnp.logical_not(alone))
+    def _():
+        col_copy.start()
+
     @pl.when(alone)
     def _():
         swap_in[...] = swap_out[...]
 
     next(inner)
-    step_all([columns])
-    col_copy = copies.start(col_unit.at[give_col], pair_in.at[1], col_partner)
-    next(inner)
-    col_copy.wait_recv()
 
     @pl.when(jnp.logical_not(alone))
     def _():
         row_copy.wait()
 
-    loads[3].wait()
-    tri = split(tri_ref[...])
-    col_rows = rows(x * UNIT + lo * PIECE, PIECE)
-    col_piece = av_col.at[col_rows]
-    col_piece[...] = product(split(col_unit[keep_col, :] + pair_in[1] + swap_in[...]), tri, NN)
-    row_copy = copies.make(col_piece, av_row.at[col // 8, col_rows], as_col)
-
-    @pl.when(jnp.logical_not(alone))
-    def _():
-        row_copy.start()
-
-    @pl.when(alone)
-    def _():
-        av_row[col // 8, col_rows, :] = col_piece[...]
-
+    av_col[rows(x * UNIT + lo * PIECE, PIECE), :] = swap_out[1] + swap_in[0]
     columns = ring_gather(copies, av_col, *x_ring, lo, col_partner)
     next(columns)
     next(inner)
+
+    @pl.when(jnp.logical_not(alone))
+    def _():
+        col_copy.wait()
+
+    av_row[core, rows(((z + row_shift) % 4) * UNIT + row_half * PIECE, PIECE), :] = swap_out[0] + swap_in[1]
+    rows_in = ring_gather(copies, av_row.at[core], *z_ring, row_half, row_partner, sibling)
+    next(rows_in)
     next(columns)
     next(inner)
-
-    @pl.when(jnp.logical_not(alone))
-    def _():
-        row_copy.wait()
-
-    rows_in = ring_gather(copies, av_row.at[core], *z_ring, row_half, row_partner, sibling)
     next(rows_in)
-    next(inner)
     next(columns)
-    next(rows_in)
     step_all([inner])
     whole_inner = inner_ref[...] + inner_ref[...].T
     middle = split(product(split(product(tri, split(whole_inner), TN)), tri, NN) * 0.5)
+    vec_middle[0] = product(whole(0), middle, NN)
+    next(rows_in)
     next(columns)
+    vec_middle[1] = product(whole(1), middle, NN)
     next(rows_in)
-    vec_middle[0] = product(whole(0), middle, NN)
     next(columns)
-    next(rows_in)
-    vec_middle[1] = product(whole(1), middle, NN)
+    vec_middle[2] = product(whole(2), middle, NN)
     step_all([columns])
     w = av_col[...] - vec_middle[0]
     w_ref[...] = w
     w_high[0], w_low[0] = split(w)
-    vec_middle[2] = product(whole(2), middle, NN)
     next(rows_in)
     step_all([rows_in])
     for position in range(2):
@@ -629,8 +626,8 @@
             buffer(UNIT, WIDTH),
             buffer(UNIT, WIDTH),
             buffer(2, PIECE, WIDTH),
-            buffer(PIECE, WIDTH),
-            buffer(PIECE, WIDTH),
+            buffer(2, PIECE, WIDTH),
+            buffer(2, PIECE, WIDTH),
             buffer(128, WIDTH),
             buffer(128, WIDTH),
             buffer(32, WIDTH),

time: 96.2 us -> 97.1 us (level)
  no operation moved by 1% of the time
where the time goes in v4:
time: 97.1 us; the launch traced here: 96.9 us
  Pallas kernels  92.6 us (95%)
  local copies, waits for them, and re-layouts  3.5 us (4%)
    pallas_call x1, Pallas kernels, shards(): pl.pallas_call(gather_kernel, out_shape=[terms, terms, terms, terms, jax....  84.7 us
    pallas_call x1, Pallas kernels, shards(): pl.pallas_call(update_kernel, out_shape=[jax.ShapeDtypeStruct(halves.shap...  7.88 us
    unnamed x8, local copies, waits for them, and re-layouts  3.5 us

profile of v4, /device:TPU:1, one launch (start us, length us, event | category | flops | bytes accessed | tf_op | source)
XLA Modules:
  0.0 96.9 jit_solution(15487221931534550908)
XLA Ops:
  0.6 0.0 copy-start
  0.6 0.0 copy-start.1
  0.7 1.1 %copy-done.1 = f32[64,1024]{1,0:T(8,128)S(1)} copy-done((f32[64,1024]{1,0:T(8,128)S(1)}, f32[64,1024]{1,0:T(8,128)}, u32[]{:S(2)}) %copy-start.1) | copy-done | bytes 262168
  1.7 0.0 copy-start.2
  1.7 1.5 %copy-done.2 = f32[1024,256]{1,0:T(8,128)S(1)} copy-done((f32[1024,256]{1,0:T(8,128)S(1)}, f32[1024,256]{1,0:T(8,128)}, u32[]{:S(2)}) %copy-start.2) | copy-done | bytes 1048600
  3.2 0.0 copy-start.3
  3.2 0.9 copy-done.3
  4.1 84.7 %gather.1 = (bf16[3,1024,256]{2,1,0:T(8,128)(2,1)S(1)}, bf16[3,1024,256]{2,1,0:T(8,128)(2,1)S(1)}, bf16[3,1024,256]{2,1,0:T(8,128)(2,1)S(1)}, bf16[3,1024,256]{2,1,0:T(8,128)(2,1)S(1)}, f32[1024,256]{1,0:T(8,128)S(1)}) custom-call(f32[2,512,1024]{2,1,0:T(8,128)} %halves_ref.3, f32[64,1024]{1,0:T(8,128)S(1)} %copy-done.1, f32[1024,256]{1,0:T(8,128)S(1)} %copy-done.2, ...), custom_call_target="tpu_custom_call" | custom-call | tf_op jit(solution)/shard_map/gather/pallas_call | solution.py:602
  88.9 0.0 copy-done
  88.9 7.9 %update.1 = (f32[2,512,1024]{2,1,0:T(8,128)}, f32[64,1024]{1,0:T(8,128)}, f32[1024,256]{1,0:T(8,128)}) custom-call(f32[2,512,1024]{2,1,0:T(8,128)S(1)} %copy-done, f32[64,1024]{1,0:T(8,128)S(1)} %copy-done.1, bf16[3,1024,256]{2,1,0:T(8,128)(2,1)S(1)} %get-tuple-element.8.vec_high, bf16[3,1024,256]{2,1,0:T(8,128)(2,1)S(1)} %get-tuple-element.9.vec_low, ...), custom_call_target="tpu_custom_call" | custom-call | tf_op jit(solution)/shard_map/update/pallas_call | solution.py:654
Async XLA Ops:
  0.6 88.2 %copy-start = (f32[2,512,1024]{2,1,0:T(8,128)S(1)}, f32[2,512,1024]{2,1,0:T(8,128)}, u32[]{:S(2)}) copy-start(f32[2,512,1024]{2,1,0:T(8,128)} %halves_ref.3) | copy-start | bytes 12582916
  0.6 1.1 %copy-start.1 = (f32[64,1024]{1,0:T(8,128)S(1)}, f32[64,1024]{1,0:T(8,128)}, u32[]{:S(2)}) copy-start(f32[64,1024]{1,0:T(8,128)} %rest_ref.1) | copy-start | bytes 786436
  1.7 1.5 %copy-start.2 = (f32[1024,256]{1,0:T(8,128)S(1)}, f32[1024,256]{1,0:T(8,128)}, u32[]{:S(2)}) copy-start(f32[1024,256]{1,0:T(8,128)} %vec_hbm.1) | copy-start | bytes 3145732
  3.2 0.9 copy-start.3

commit v5 on v4

--- a/solution.py
+++ b/solution.py
@@ -276,43 +276,38 @@
 
 
 def inner_sum(copies, me, partial, total, work):
-    first, first_in, second, second_in, third, third_in, fourth_in, fifth, sixth = work
+    first, first_in, second_in, third_in, fourth_in = work
     sibling = moved(me, core=1)
-    core, x, y = me["core"], me["x"], me["hi"] * 2 + me["lo"]
+    core, x, y, z = me["core"], me["x"], me["hi"] * 2 + me["lo"], me["z"]
     copy = copies.start(partial.at[rows((1 - core) * 128, 128)], first_in, sibling)
     yield
     copy.wait_recv()
     first[...] = partial[rows(core * 128, 128), :] + first_in[...]
     sent = [
-        copies.start(first.at[rows(((x + d) % 4) * 32, 32)], second_in.at[d - 1], moved(me, x=d)) for d in (1, 2, 3)
+        copies.start(first.at[rows(((y + d) % 4) * 32, 32)], second_in.at[d - 1], moved(me, y=d)) for d in (1, 2, 3)
     ]
     yield
     for copy in sent:
         copy.wait_recv()
-    second[...] = first[rows(x * 32, 32), :] + second_in[0] + second_in[1] + second_in[2]
-    sent = [copies.start(second.at[rows(((y + d) % 4) * 8, 8)], third_in.at[d - 1], moved(me, y=d)) for d in (1, 2, 3)]
+    mine = third_in.at[z]
+    mine[...] = first[rows(y * 32, 32), :] + second_in[0] + second_in[1] + second_in[2]
+    sent = [copies.start(mine, mine, moved(me, z=d)) for d in (1, 2, 3)]
     yield
     for copy in sent:
         copy.wait_recv()
-    third[...] = second[rows(y * 8, 8), :] + third_in[0] + third_in[1] + third_in[2]
-    sent = [copies.start(third, fourth_in.at[d - 1], moved(me, z=d)) for d in (1, 2, 3)]
+    mine = fourth_in.at[x]
+    mine[...] = third_in[0] + third_in[1] + third_in[2] + third_in[3]
+    sent = [copies.start(mine, mine, moved(me, x=d)) for d in (1, 2, 3)]
     yield
     for copy in sent:
         copy.wait_recv()
-    mine = fifth.at[rows(y * 8, 8)]
-    mine[...] = third[...] + fourth_in[0] + fourth_in[1] + fourth_in[2]
+    mine = total.at[rows(core * 128 + y * 32, 32)]
+    mine[...] = fourth_in[0] + fourth_in[1] + fourth_in[2] + fourth_in[3]
     sent = [copies.start(mine, mine, moved(me, y=d)) for d in (1, 2, 3)]
-    yield
-    for copy in sent:
-        copy.wait_recv()
-    mine = sixth.at[rows(x * 32, 32)]
-    mine[...] = fifth[...]
-    sent = [copies.start(mine, mine, moved(me, x=d)) for d in (1, 2, 3)]
     yield
     for copy in sent:
         copy.wait_recv()
     mine = total.at[rows(core * 128, 128)]
-    mine[...] = sixth[...]
     copy = copies.start(mine, mine, sibling)
     yield
     copy.wait_recv()
@@ -331,7 +326,7 @@
     vec_ref, rest_ref, tri_ref, av_col, av_row, vec_row, inner_ref, vec_middle,
     tiles, tile_high, tile_low, parts, rest_part, partial, row_sum, sibling_in, row_relay, col_relay,
     row_unit, col_unit, pair_in, swap_out, swap_in,
-    first, first_in, second, second_in, third, third_in, fourth_in, fifth, sixth,
+    first, first_in, second_in, third_in, fourth_in,
     load_sems, send_sems, recv_sems, vec_send_sems, vec_recv_sems,
 ):
     me = place()
@@ -446,7 +441,7 @@
     columns = ring_scatter(copies, parts.at[0], col_unit, col_relay, *x_ring)
     next(columns)
     inner = inner_sum(
-        copies, me, partial, inner_ref, (first, first_in, second, second_in, third, third_in, fourth_in, fifth, sixth)
+        copies, me, partial, inner_ref, (first, first_in, second_in, third_in, fourth_in)
     )
     next(inner)
     loads[3].wait()
@@ -460,10 +455,11 @@
     give_row, give_col = rows((1 - row_half) * PIECE, PIECE), rows((1 - lo) * PIECE, PIECE)
     row_partner = moved(me, y=2)
     col_partner = at(x, 1 - lo, z, hi, core)
+    next(inner)
     row_copy = copies.start(row_unit.at[give_row], pair_in.at[0], row_partner)
-    next(inner)
     step_all([columns])
     col_copy = copies.start(col_unit.at[give_col], pair_in.at[1], col_partner)
+    next(inner)
     row_copy.wait_recv()
     swap_out[0] = product(split(row_unit[keep_row, :] + pair_in[0]), tri, NN)
     row_copy = copies.make(swap_out.at[0], swap_in.at[0], as_row)
@@ -472,7 +468,6 @@
     def _():
         row_copy.start()
 
-    next(inner)
     col_copy.wait_recv()
     swap_out[1] = product(split(col_unit[keep_col, :] + pair_in[1]), tri, NN)
     col_copy = copies.make(swap_out.at[1], swap_in.at[1], as_col)
@@ -504,10 +499,9 @@
     rows_in = ring_gather(copies, av_row.at[core], *z_ring, row_half, row_partner, sibling)
     next(rows_in)
     next(columns)
-    next(inner)
+    step_all([inner])
     next(rows_in)
     next(columns)
-    step_all([inner])
     whole_inner = inner_ref[...] + inner_ref[...].T
     middle = split(product(split(product(tri, split(whole_inner), TN)), tri, NN) * 0.5)
     vec_middle[0] = product(whole(0), middle, NN)
@@ -598,6 +592,8 @@
     def buffer(*shape):
         return pltpu.VMEM(shape, f32)
 
+    held = pltpu.with_memory_space_constraint
+    diag_rest, panel_vectors, tri_factor = (held(value, pltpu.HBM) for value in (diag_rest, panel_vectors, tri_factor))
     terms = jax.ShapeDtypeStruct((3,) + block, jnp.bfloat16)
     handed = pl.pallas_call(
         gather_kernel,
@@ -630,13 +626,9 @@
             buffer(2, PIECE, WIDTH),
             buffer(128, WIDTH),
             buffer(128, WIDTH),
-            buffer(32, WIDTH),
             buffer(3, 32, WIDTH),
-            buffer(8, WIDTH),
-            buffer(3, 8, WIDTH),
-            buffer(3, 8, WIDTH),
-            buffer(32, WIDTH),
-            buffer(128, WIDTH),
+            buffer(4, 32, WIDTH),
+            buffer(4, 32, WIDTH),
             pltpu.SemaphoreType.DMA((4,)),
             pltpu.SemaphoreType.DMA((80,)),
             pltpu.SemaphoreType.DMA((80,)),

time: 97.1 us -> 93.4 us (0.962)
  local copies, waits for them, and re-layouts: 3.5 us -> 0.01 us
    unnamed x8 -> x2, local copies, waits for them, and re-layouts: 3.5 us -> 0.01 us
where the time goes in v5:
time: 93.4 us; the launch traced here: 93.3 us
  Pallas kernels  92.5 us (99%)
    pallas_call x1, Pallas kernels, shards(): pl.pallas_call(gather_kernel, out_shape=[terms, terms, terms, terms, jax....  84.6 us
    pallas_call x1, Pallas kernels, shards(): pl.pallas_call(update_kernel, out_shape=[jax.ShapeDtypeStruct(halves.shap...  7.86 us

profile of v5, /device:TPU:1, one launch (start us, length us, event | category | flops | bytes accessed | tf_op | source)
XLA Modules:
  0.0 93.3 jit_solution(6938251970865861726)
XLA Ops:
  0.6 0.0 copy-start
  0.6 84.6 %gather.1 = (bf16[3,1024,256]{2,1,0:T(8,128)(2,1)S(1)}, bf16[3,1024,256]{2,1,0:T(8,128)(2,1)S(1)}, bf16[3,1024,256]{2,1,0:T(8,128)(2,1)S(1)}, bf16[3,1024,256]{2,1,0:T(8,128)(2,1)S(1)}, f32[1024,256]{1,0:T(8,128)S(1)}) custom-call(f32[2,512,1024]{2,1,0:T(8,128)} %halves_ref.3, f32[64,1024]{1,0:T(8,128)} %rest_ref.1, f32[1024,256]{1,0:T(8,128)} %vec_hbm.1, ...), custom_call_target="tpu_custom_call" | custom-call | tf_op jit(solution)/shard_map/gather/pallas_call | solution.py:598
  85.3 0.0 copy-done
  85.3 7.9 %update.1 = (f32[2,512,1024]{2,1,0:T(8,128)}, f32[64,1024]{1,0:T(8,128)}, f32[1024,256]{1,0:T(8,128)}) custom-call(f32[2,512,1024]{2,1,0:T(8,128)S(1)} %copy-done, f32[64,1024]{1,0:T(8,128)} %rest_ref.1, bf16[3,1024,256]{2,1,0:T(8,128)(2,1)S(1)} %get-tuple-element.8.vec_high, bf16[3,1024,256]{2,1,0:T(8,128)(2,1)S(1)} %get-tuple-element.9.vec_low, ...), custom_call_target="tpu_custom_call" | custom-call | tf_op jit(solution)/shard_map/update/pallas_call | solution.py:646
Async XLA Ops:
  0.6 84.6 %copy-start = (f32[2,512,1024]{2,1,0:T(8,128)S(1)}, f32[2,512,1024]{2,1,0:T(8,128)}, u32[]{:S(2)}) copy-start(f32[2,512,1024]{2,1,0:T(8,128)} %halves_ref.3) | copy-start | bytes 12582916

commit v6 on v5

--- a/solution.py
+++ b/solution.py
@@ -108,6 +108,10 @@
     given = 1 - kept
     shared = []
 
+    def part(step, which, at_half):
+        start = ((index + step + shift) % 4) * UNIT + which * PIECE + at_half * (PIECE // 2)
+        return block.at[rows(start, PIECE // 2)]
+
     def share(ref):
         if sibling is not None:
             shared.append(copies.start(ref, ref, sibling))
@@ -116,14 +120,16 @@
         return copies.start(ref, ref, device)
 
     own = piece(0, kept)
-    pair = send(own, partner)
+    pair = [send(part(0, kept, half), partner) for half in (0, 1)]
     own_plus, own_minus = send(own, plus), send(own, minus)
     share(own)
     yield
-    pair.wait_recv()
-    other = piece(0, given)
-    other_plus, other_minus = send(other, plus), send(other, minus)
-    share(other)
+    other_plus, other_minus = [], []
+    for half in (0, 1):
+        pair[half].wait_recv()
+        other_minus.append(send(part(0, given, half), minus))
+        other_plus.append(send(part(0, given, half), plus))
+    share(piece(0, given))
     yield
     own_plus.wait_recv()
     far_plus = send(piece(3, kept), plus)
@@ -131,22 +137,28 @@
     own_minus.wait_recv()
     share(piece(1, kept))
     yield
-    other_minus.wait_recv()
-    far_minus = send(piece(1, given), minus)
+    far_minus = []
+    for half in (0, 1):
+        other_minus[half].wait_recv()
+        far_minus.append(send(part(1, given, half), minus))
     share(piece(1, given))
-    other_plus.wait_recv()
+    for copy in other_plus:
+        copy.wait_recv()
     share(piece(3, given))
     yield
     far_plus.wait_recv()
     share(piece(2, kept))
-    far_minus.wait_recv()
-    share(piece(2, given))
+    for half in (0, 1):
+        far_minus[half].wait_recv()
+        share(part(2, given, half))
     yield
     for copy in shared:
         copy.wait_recv()
 
 
-ORDER = (0, 4, 1, 5, 2, 6, 3, 7)
+CHUNKS = 16
+CHUNK = TILE // CHUNKS
+ORDER = [half + c for c in range(CHUNKS // 2) for half in (0, CHUNKS // 2)]
 
 
 class Spread:
@@ -168,7 +180,7 @@
         self.from_minus = ((z + 3) % 4) // 2
 
     def chunk(self, block, c):
-        return self.vec_row.at[block, pl.ds(c * PIECE, PIECE)]
+        return self.vec_row.at[block, pl.ds(c * CHUNK, CHUNK)]
 
     def copy(self, slot, source, target, device):
         return pltpu.make_async_remote_copy(
@@ -181,7 +193,7 @@
         )
 
     def mine(self, c):
-        return self.vec_ref.at[pl.ds(c * PIECE, PIECE)]
+        return self.vec_ref.at[pl.ds(c * CHUNK, CHUNK)]
 
     def along(self, c, block, source=None):
         here = self.chunk(block, c)
@@ -189,14 +201,14 @@
 
     def back(self, c, block, source=None):
         here = self.chunk(block, c)
-        return self.copy(8 + c, here if source is None else source, here, self.minus)
+        return self.copy(CHUNKS + c, here if source is None else source, here, self.minus)
 
     def across(self, c):
-        return self.copy(16 + c, self.mine(c), self.chunk(self.own, c), self.over)
+        return self.copy(2 * CHUNKS + c, self.mine(c), self.chunk(self.own, c), self.over)
 
     def share(self, c, block, which, source=None):
         here = self.chunk(block, c)
-        return self.copy(24 + 8 * which + c, here if source is None else source, here, self.sibling)
+        return self.copy((3 + which) * CHUNKS + c, here if source is None else source, here, self.sibling)
 
     def begin(self):
         @pl.when(self.source)
@@ -212,9 +224,12 @@
             for c in ORDER:
                 self.across(c).start()
 
-    def serve(self, step):
-        c = ORDER[step]
-
+    def serve(self, *steps):
+        for step in steps:
+            self.pass_on(ORDER[2 * step])
+            self.pass_on(ORDER[2 * step + 1])
+
+    def pass_on(self, c):
         @pl.when(self.target)
         def _():
             self.across(c).wait_recv()
@@ -226,11 +241,11 @@
         def _():
             block = self.from_minus
             self.along(c, block).wait_recv()
-            if c < 4:
+            if c < CHUNKS // 2:
                 self.along(c, block).start()
             self.share(c, block, 0).start()
             self.back(c, 1 - block).wait_recv()
-            if c >= 4:
+            if c >= CHUNKS // 2:
                 self.back(c, 1 - block).start()
             self.share(c, 1 - block, 1).start()
 
@@ -238,7 +253,7 @@
         @pl.when(self.ends)
         def _():
             for c in ORDER:
-                copy = self.along(c, 1 - self.own) if c < 4 else self.back(c, 1 - self.own)
+                copy = self.along(c, 1 - self.own) if c < CHUNKS // 2 else self.back(c, 1 - self.own)
                 copy.wait_recv()
                 self.share(c, 1 - self.own, 1).start()
 
@@ -258,7 +273,7 @@
         @pl.when(self.middle)
         def _():
             for c in ORDER:
-                if c < 4:
+                if c < CHUNKS // 2:
                     self.along(c, 0).wait_send()
                 else:
                     self.back(c, 0).wait_send()
@@ -324,7 +339,7 @@
 def gather_kernel(
     halves_ref, rest_hbm, vec_hbm, tri_hbm, vec_high, vec_low, w_high, w_low, w_ref,
     vec_ref, rest_ref, tri_ref, av_col, av_row, vec_row, inner_ref, vec_middle,
-    tiles, tile_high, tile_low, parts, rest_part, partial, row_sum, sibling_in, row_relay, col_relay,
+    tiles, tile_high, tile_low, col_high, col_low, parts, rest_part, partial, row_sum, sibling_in, row_relay, col_relay,
     row_unit, col_unit, pair_in, swap_out, swap_in,
     first, first_in, second_in, third_in, fourth_in,
     load_sems, send_sems, recv_sems, vec_send_sems, vec_recv_sems,
@@ -436,10 +451,11 @@
     col_part(0)
     vec_high[2], vec_low[2] = split(vec_row[1])
     col_part(1)
-    partial[...] = product(whole(0), split(parts[0]), TN)
+    col_high[...], col_low[...] = split(parts[0])
     parts[0, rest_rows, :] += rest_part[...]
     columns = ring_scatter(copies, parts.at[0], col_unit, col_relay, *x_ring)
     next(columns)
+    partial[...] = product(whole(0), (col_high[...], col_low[...]), TN)
     inner = inner_sum(
         copies, me, partial, inner_ref, (first, first_in, second_in, third_in, fourth_in)
     )
@@ -612,6 +628,8 @@
             buffer(2, HALF, TILE),
             pltpu.VMEM((2, HALF, TILE), jnp.bfloat16),
             pltpu.VMEM((2, HALF, TILE), jnp.bfloat16),
+            pltpu.VMEM(block, jnp.bfloat16),
+            pltpu.VMEM(block, jnp.bfloat16),
             buffer(3, *block),
             buffer(REST, WIDTH),
             buffer(WIDTH, WIDTH),
@@ -632,8 +650,8 @@
             pltpu.SemaphoreType.DMA((4,)),
             pltpu.SemaphoreType.DMA((80,)),
             pltpu.SemaphoreType.DMA((80,)),
-            pltpu.SemaphoreType.DMA((40,)),
-            pltpu.SemaphoreType.DMA((40,)),
+            pltpu.SemaphoreType.DMA((5 * CHUNKS,)),
+            pltpu.SemaphoreType.DMA((5 * CHUNKS,)),
         ],
         compiler_params=pltpu.CompilerParams(
             collective_id=0, has_side_effects=True, vmem_limit_bytes=44 * 2**20

time: 93.4 us -> 90.7 us (0.971)
  Pallas kernels: 92.5 us -> 89.7 us
    pallas_call x1, Pallas kernels: 84.6 us -> 81.9 us  [shards(): pl.pallas_call(gather_kernel, out_shape=[terms, terms, terms, terms, jax....]
where the time goes in v6:
time: 90.7 us; the launch traced here: 90.6 us
  Pallas kernels  89.7 us (99%)
    pallas_call x1, Pallas kernels, shards(): pl.pallas_call(gather_kernel, out_shape=[terms, terms, terms, terms, jax....  81.9 us
    pallas_call x1, Pallas kernels, shards(): pl.pallas_call(update_kernel, out_shape=[jax.ShapeDtypeStruct(halves.shap...  7.86 us

profile of v6, /device:TPU:1, one launch (start us, length us, event | category | flops | bytes accessed | tf_op | source)
XLA Modules:
  0.0 90.6 jit_solution(4850031061599630916)
XLA Ops:
  0.6 0.0 copy-start
  0.6 81.9 %gather.1 = (bf16[3,1024,256]{2,1,0:T(8,128)(2,1)S(1)}, bf16[3,1024,256]{2,1,0:T(8,128)(2,1)S(1)}, bf16[3,1024,256]{2,1,0:T(8,128)(2,1)S(1)}, bf16[3,1024,256]{2,1,0:T(8,128)(2,1)S(1)}, f32[1024,256]{1,0:T(8,128)S(1)}) custom-call(f32[2,512,1024]{2,1,0:T(8,128)} %halves_ref.3, f32[64,1024]{1,0:T(8,128)} %rest_ref.1, f32[1024,256]{1,0:T(8,128)} %vec_hbm.1, ...), custom_call_target="tpu_custom_call" | custom-call | tf_op jit(solution)/shard_map/gather/pallas_call | solution.py:614
  82.5 0.0 copy-done
  82.5 7.9 %update.1 = (f32[2,512,1024]{2,1,0:T(8,128)}, f32[64,1024]{1,0:T(8,128)}, f32[1024,256]{1,0:T(8,128)}) custom-call(f32[2,512,1024]{2,1,0:T(8,128)S(1)} %copy-done, f32[64,1024]{1,0:T(8,128)} %rest_ref.1, bf16[3,1024,256]{2,1,0:T(8,128)(2,1)S(1)} %get-tuple-element.8.vec_high, bf16[3,1024,256]{2,1,0:T(8,128)(2,1)S(1)} %get-tuple-element.9.vec_low, ...), custom_call_target="tpu_custom_call" | custom-call | tf_op jit(solution)/shard_map/update/pallas_call | solution.py:664
Async XLA Ops:
  0.6 81.9 %copy-start = (f32[2,512,1024]{2,1,0:T(8,128)S(1)}, f32[2,512,1024]{2,1,0:T(8,128)}, u32[]{:S(2)}) copy-start(f32[2,512,1024]{2,1,0:T(8,128)} %halves_ref.3) | copy-start | bytes 12582916

commit v7 on v6

--- a/solution.py
+++ b/solution.py
@@ -77,28 +77,54 @@
             copy.wait_send()
 
 
-def ring_scatter(copies, source, out, relay, index, shift, plus, minus):
-    def part(step, half):
-        return source.at[rows(((index + step + shift) % 4) * UNIT + half * PIECE, PIECE)]
-
-    far_plus = copies.start(part(2, 0), relay.at[0], plus)
-    far_minus = copies.start(part(2, 1), relay.at[1], minus)
-    near_plus = copies.start(part(1, 1), relay.at[2], plus)
-    near_minus = copies.start(part(3, 0), relay.at[3], minus)
-    yield
-    far_plus.wait_recv()
-    relay[6] = relay[0] + part(1, 0)[...]
-    sum_plus = copies.start(relay.at[6], relay.at[4], plus)
-    far_minus.wait_recv()
-    relay[7] = relay[1] + part(3, 1)[...]
-    sum_minus = copies.start(relay.at[7], relay.at[5], minus)
-    yield
-    near_plus.wait_recv()
-    near_minus.wait_recv()
-    sum_plus.wait_recv()
-    sum_minus.wait_recv()
-    out[0:PIECE] = part(0, 0)[...] + (relay[4] + relay[3])
-    out[PIECE:UNIT] = part(0, 1)[...] + (relay[2] + relay[5])
+def ring_scatter(copies, source, out, relay, index, shift, plus, minus, kept, partner, pair_in):
+    size = PIECE // 2
+    given = 1 - kept
+
+    def part(step, which, at_half):
+        return source.at[rows(((index + step + shift) % 4) * UNIT + which * PIECE + at_half * size, size)]
+
+    def far(base, which):
+        return (
+            copies.start(part(2, which, 0), relay.at[base], plus),
+            copies.start(part(2, which, 1), relay.at[base + 1], minus),
+        )
+
+    def near(base, which):
+        return (
+            copies.start(part(1, which, 1), relay.at[base + 2], plus),
+            copies.start(part(3, which, 0), relay.at[base + 3], minus),
+        )
+
+    def passed(base, which, arriving):
+        arriving[0].wait_recv()
+        relay[base + 6] = relay[base] + part(1, which, 0)[...]
+        to_plus = copies.start(relay.at[base + 6], relay.at[base + 4], plus)
+        arriving[1].wait_recv()
+        relay[base + 7] = relay[base + 1] + part(3, which, 1)[...]
+        return to_plus, copies.start(relay.at[base + 7], relay.at[base + 5], minus)
+
+    def total(base, which, arriving):
+        for copy in arriving:
+            copy.wait_recv()
+        out[rows(which * PIECE, size), :] = part(0, which, 0)[...] + (relay[base + 4] + relay[base + 3])
+        out[rows(which * PIECE + size, size), :] = part(0, which, 1)[...] + (relay[base + 2] + relay[base + 5])
+
+    far_given = far(0, given)
+    near_given = near(0, given)
+    far_kept = far(8, kept)
+    yield
+    sum_given = passed(0, given, far_given)
+    near_kept = near(8, kept)
+    yield
+    sum_kept = passed(8, kept, far_kept)
+    yield
+    total(0, given, near_given + sum_given)
+    pair = copies.start(out.at[rows(given * PIECE, PIECE)], pair_in, partner)
+    yield
+    total(8, kept, near_kept + sum_kept)
+    yield
+    pair.wait_recv()
 
 
 def ring_gather(copies, block, index, shift, plus, minus, kept, partner, sibling=None):
@@ -426,6 +452,8 @@
         def _():
             parts[0, HALF:TILE] += product((tile[0][...], tile[1][...]), whole(1 + position), NN)
 
+    row_partner = moved(me, y=2)
+    col_partner = at(x, 1 - lo, z, hi, core)
     row_part(1 - core)
     pair = copies.start(parts.at[2 - core], sibling_in, sibling)
     spread.serve(0)
@@ -442,7 +470,7 @@
     pair.wait_recv()
     row_sum[...] = parts[1 + core] + sibling_in[...]
     spread.serve(5)
-    row_scatter = ring_scatter(copies, row_sum, row_unit, row_relay, *z_ring)
+    row_scatter = ring_scatter(copies, row_sum, row_unit, row_relay, *z_ring, row_half, row_partner, pair_in.at[0])
     next(row_scatter)
     spread.serve(6)
     spread.serve(7)
@@ -453,7 +481,7 @@
     col_part(1)
     col_high[...], col_low[...] = split(parts[0])
     parts[0, rest_rows, :] += rest_part[...]
-    columns = ring_scatter(copies, parts.at[0], col_unit, col_relay, *x_ring)
+    columns = ring_scatter(copies, parts.at[0], col_unit, col_relay, *x_ring, lo, col_partner, pair_in.at[1])
     next(columns)
     partial[...] = product(whole(0), (col_high[...], col_low[...]), TN)
     inner = inner_sum(
@@ -464,19 +492,15 @@
     tri = split(tri_ref[...])
     next(row_scatter)
     next(inner)
+    next(row_scatter)
+    next(columns)
+    next(row_scatter)
+    next(columns)
+    next(row_scatter)
+    next(inner)
     next(columns)
     step_all([row_scatter])
-
     keep_row, keep_col = rows(row_half * PIECE, PIECE), rows(lo * PIECE, PIECE)
-    give_row, give_col = rows((1 - row_half) * PIECE, PIECE), rows((1 - lo) * PIECE, PIECE)
-    row_partner = moved(me, y=2)
-    col_partner = at(x, 1 - lo, z, hi, core)
-    next(inner)
-    row_copy = copies.start(row_unit.at[give_row], pair_in.at[0], row_partner)
-    step_all([columns])
-    col_copy = copies.start(col_unit.at[give_col], pair_in.at[1], col_partner)
-    next(inner)
-    row_copy.wait_recv()
     swap_out[0] = product(split(row_unit[keep_row, :] + pair_in[0]), tri, NN)
     row_copy = copies.make(swap_out.at[0], swap_in.at[0], as_row)
 
@@ -484,7 +508,9 @@
     def _():
         row_copy.start()
 
-    col_copy.wait_recv()
+    next(columns)
+    next(inner)
+    step_all([columns])
     swap_out[1] = product(split(col_unit[keep_col, :] + pair_in[1]), tri, NN)
     col_copy = copies.make(swap_out.at[1], swap_in.at[1], as_col)
 
@@ -541,7 +567,7 @@
 
 def update_kernel(
     halves_ref, rest_ref, vec_high, vec_low, w_high, w_low, w_ref, out_ref, out_rest, out_w,
-    tiles, rest, load_sems, store_sems, side_sems,
+    tiles, rest, store_sems, side_sems,
 ):
     row, col = lax.axis_index("row"), lax.axis_index("col")
     count, _, size = tiles.shape
@@ -550,19 +576,21 @@
     def place_of(ref, at_step):
         return ref.at[at_step // each, :, pl.ds(pl.multiple_of((at_step % each) * size, size), size)]
 
-    def load(at_step):
-        return pltpu.make_async_copy(place_of(halves_ref, at_step), tiles.at[at_step], load_sems.at[at_step])
-
     def store(at_step):
         return pltpu.make_async_copy(tiles.at[at_step], place_of(out_ref, at_step), store_sems.at[at_step])
 
     w_copy = pltpu.make_async_copy(w_ref, out_w, side_sems.at[0])
     rest_in = pltpu.make_async_copy(rest_ref, rest, side_sems.at[1])
     rest_out = pltpu.make_async_copy(rest, out_rest, side_sems.at[2])
-    for at_step in range(count):
-        load(at_step).start()
     rest_in.start()
     w_copy.start()
+    rest_rows = rows(HALF + row * REST, REST)
+    update = product(
+        (vec_high[0, rest_rows, :], vec_low[0, rest_rows, :]), (w_high[0], w_low[0]), NT
+    ) + product((w_high[0, rest_rows, :], w_low[0, rest_rows, :]), (vec_high[0], vec_low[0]), NT)
+    rest_in.wait()
+    rest[...] = rest[...] - update
+    rest_out.start()
 
     def one(at_step, carry):
         position = at_step // each
@@ -580,19 +608,11 @@
             (vec_high[low_at, low_rows, :], vec_low[low_at, low_rows, :]),
             NT,
         )
-        load(at_step).wait()
-        tiles[at_step] = tiles[at_step] - update
+        tiles[at_step] = place_of(halves_ref, at_step)[...] - update
         store(at_step).start()
         return carry
 
     lax.fori_loop(0, count, one, 0)
-    rest_rows = rows(HALF + row * REST, REST)
-    update = product(
-        (vec_high[0, rest_rows, :], vec_low[0, rest_rows, :]), (w_high[0], w_low[0]), NT
-    ) + product((w_high[0, rest_rows, :], w_low[0, rest_rows, :]), (vec_high[0], vec_low[0]), NT)
-    rest_in.wait()
-    rest[...] = rest[...] - update
-    rest_out.start()
     for at_step in range(count):
         store(at_step).wait()
     w_copy.wait()
@@ -635,8 +655,8 @@
             buffer(WIDTH, WIDTH),
             buffer(*block),
             buffer(*block),
-            buffer(8, PIECE, WIDTH),
-            buffer(8, PIECE, WIDTH),
+            buffer(16, PIECE // 2, WIDTH),
+            buffer(16, PIECE // 2, WIDTH),
             buffer(UNIT, WIDTH),
             buffer(UNIT, WIDTH),
             buffer(2, PIECE, WIDTH),
@@ -648,8 +668,8 @@
             buffer(4, 32, WIDTH),
             buffer(4, 32, WIDTH),
             pltpu.SemaphoreType.DMA((4,)),
-            pltpu.SemaphoreType.DMA((80,)),
-            pltpu.SemaphoreType.DMA((80,)),
+            pltpu.SemaphoreType.DMA((96,)),
+            pltpu.SemaphoreType.DMA((96,)),
             pltpu.SemaphoreType.DMA((5 * CHUNKS,)),
             pltpu.SemaphoreType.DMA((5 * CHUNKS,)),
         ],
@@ -668,12 +688,11 @@
             jax.ShapeDtypeStruct(diag_rest.shape, f32),
             jax.ShapeDtypeStruct(panel_vectors.shape, f32),
         ],
-        in_specs=[outside] * 2 + [vmem] * 5,
+        in_specs=[vmem, outside] + [vmem] * 5,
         out_specs=[outside] * 3,
         scratch_shapes=[
             buffer(count, HALF, size),
             buffer(REST, TILE),
-            pltpu.SemaphoreType.DMA((count,)),
             pltpu.SemaphoreType.DMA((count,)),
             pltpu.SemaphoreType.DMA((3,)),
         ],

time: 90.7 us -> 85.3 us (0.940); the launches traced: 90.6 us -> 84.1 us
  Pallas kernels: 89.7 us -> 83.2 us
    pallas_call x1, Pallas kernels: 81.9 us -> 76.3 us  [shards(): pl.pallas_call(gather_kernel, out_shape=[terms, terms, terms, terms, jax....]
    pallas_call x1, Pallas kernels: 7.86 us -> 6.94 us  [shards(): pl.pallas_call(update_kernel, out_shape=[jax.ShapeDtypeStruct(halves.shap...]
where the time goes in v7:
time: 85.3 us; the launch traced here: 84.1 us
  Pallas kernels  83.2 us (98%)
    pallas_call x1, Pallas kernels, shards(): pl.pallas_call(gather_kernel, out_shape=[terms, terms, terms, terms, jax....  76.3 us
    pallas_call x1, Pallas kernels, shards(): pl.pallas_call(update_kernel, out_shape=[jax.ShapeDtypeStruct(halves.shap...  6.94 us

profile of v7, /device:TPU:1, one launch (start us, length us, event | category | flops | bytes accessed | tf_op | source)
XLA Modules:
  0.0 84.1 jit_solution(4734066125348950180)
XLA Ops:
  0.6 0.0 copy-start
  0.6 76.3 %gather.1 = (bf16[3,1024,256]{2,1,0:T(8,128)(2,1)S(1)}, bf16[3,1024,256]{2,1,0:T(8,128)(2,1)S(1)}, bf16[3,1024,256]{2,1,0:T(8,128)(2,1)S(1)}, bf16[3,1024,256]{2,1,0:T(8,128)(2,1)S(1)}, f32[1024,256]{1,0:T(8,128)S(1)}) custom-call(f32[2,512,1024]{2,1,0:T(8,128)} %halves_ref.3, f32[64,1024]{1,0:T(8,128)} %rest_ref.1, f32[1024,256]{1,0:T(8,128)} %vec_hbm.1, ...), custom_call_target="tpu_custom_call" | custom-call | tf_op jit(solution)/shard_map/gather/pallas_call | solution.py:634
  76.9 0.0 copy-done
  76.9 6.9 %update.1 = (f32[2,512,1024]{2,1,0:T(8,128)}, f32[64,1024]{1,0:T(8,128)}, f32[1024,256]{1,0:T(8,128)}) custom-call(f32[2,512,1024]{2,1,0:T(8,128)S(1)} %copy-done, f32[64,1024]{1,0:T(8,128)} %rest_ref.1, bf16[3,1024,256]{2,1,0:T(8,128)(2,1)S(1)} %get-tuple-element.8.vec_high, bf16[3,1024,256]{2,1,0:T(8,128)(2,1)S(1)} %get-tuple-element.9.vec_low, ...), custom_call_target="tpu_custom_call" | custom-call | tf_op jit(solution)/shard_map/update/pallas_call | solution.py:684
Async XLA Ops:
  0.6 76.3 %copy-start = (f32[2,512,1024]{2,1,0:T(8,128)S(1)}, f32[2,512,1024]{2,1,0:T(8,128)}, u32[]{:S(2)}) copy-start(f32[2,512,1024]{2,1,0:T(8,128)} %halves_ref.3) | copy-start | bytes 12582916

commit v8 on v7

--- a/solution.py
+++ b/solution.py
@@ -470,11 +470,11 @@
     pair.wait_recv()
     row_sum[...] = parts[1 + core] + sibling_in[...]
     spread.serve(5)
-    row_scatter = ring_scatter(copies, row_sum, row_unit, row_relay, *z_ring, row_half, row_partner, pair_in.at[0])
-    next(row_scatter)
     spread.serve(6)
     spread.serve(7)
     spread.end()
+    row_scatter = ring_scatter(copies, row_sum, row_unit, row_relay, *z_ring, row_half, row_partner, pair_in.at[0])
+    next(row_scatter)
     vec_high[1], vec_low[1] = split(vec_row[0])
     col_part(0)
     vec_high[2], vec_low[2] = split(vec_row[1])

time: 85.3 us -> 81.2 us (0.952); the launches traced: 84.1 us -> 81.1 us
  Pallas kernels: 83.2 us -> 80.3 us
    pallas_call x1, Pallas kernels: 76.3 us -> 73.3 us  [shards(): pl.pallas_call(gather_kernel, out_shape=[terms, terms, terms, terms, jax....]
where the time goes in v8:
time: 81.2 us; the launch traced here: 81.1 us
  Pallas kernels  80.3 us (99%)
    pallas_call x1, Pallas kernels, shards(): pl.pallas_call(gather_kernel, out_shape=[terms, terms, terms, terms, jax....  73.3 us
    pallas_call x1, Pallas kernels, shards(): pl.pallas_call(update_kernel, out_shape=[jax.ShapeDtypeStruct(halves.shap...  6.94 us

profile of v8, /device:TPU:1, one launch (start us, length us, event | category | flops | bytes accessed | tf_op | source)
XLA Modules:
  0.0 81.1 jit_solution(5472643634585158790)
XLA Ops:
  0.6 0.0 copy-start
  0.6 73.3 %gather.1 = (bf16[3,1024,256]{2,1,0:T(8,128)(2,1)S(1)}, bf16[3,1024,256]{2,1,0:T(8,128)(2,1)S(1)}, bf16[3,1024,256]{2,1,0:T(8,128)(2,1)S(1)}, bf16[3,1024,256]{2,1,0:T(8,128)(2,1)S(1)}, f32[1024,256]{1,0:T(8,128)S(1)}) custom-call(f32[2,512,1024]{2,1,0:T(8,128)} %halves_ref.3, f32[64,1024]{1,0:T(8,128)} %rest_ref.1, f32[1024,256]{1,0:T(8,128)} %vec_hbm.1, ...), custom_call_target="tpu_custom_call" | custom-call | tf_op jit(solution)/shard_map/gather/pallas_call | solution.py:634
  74.0 0.0 copy-done
  74.0 6.9 %update.1 = (f32[2,512,1024]{2,1,0:T(8,128)}, f32[64,1024]{1,0:T(8,128)}, f32[1024,256]{1,0:T(8,128)}) custom-call(f32[2,512,1024]{2,1,0:T(8,128)S(1)} %copy-done, f32[64,1024]{1,0:T(8,128)} %rest_ref.1, bf16[3,1024,256]{2,1,0:T(8,128)(2,1)S(1)} %get-tuple-element.8.vec_high, bf16[3,1024,256]{2,1,0:T(8,128)(2,1)S(1)} %get-tuple-element.9.vec_low, ...), custom_call_target="tpu_custom_call" | custom-call | tf_op jit(solution)/shard_map/update/pallas_call | solution.py:684
Async XLA Ops:
  0.6 73.3 %copy-start = (f32[2,512,1024]{2,1,0:T(8,128)S(1)}, f32[2,512,1024]{2,1,0:T(8,128)}, u32[]{:S(2)}) copy-start(f32[2,512,1024]{2,1,0:T(8,128)} %halves_ref.3) | copy-start | bytes 12582916

commit v9 on v8

--- a/solution.py
+++ b/solution.py
@@ -204,6 +204,7 @@
         self.over = at(x, core, z, 1 - hi, core)
         self.own = z // 2
         self.from_minus = ((z + 3) % 4) // 2
+        self.early = jnp.where(end, self.own, self.from_minus)
 
     def chunk(self, block, c):
         return self.vec_row.at[block, pl.ds(c * CHUNK, CHUNK)]
@@ -275,6 +276,12 @@
                 self.back(c, 1 - block).start()
             self.share(c, 1 - block, 1).start()
 
+    def half_end(self):
+        @pl.when(self.follow)
+        def _():
+            for c in ORDER:
+                self.share(c, 0, 0).wait_recv()
+
     def end(self):
         @pl.when(self.ends)
         def _():
@@ -286,8 +293,7 @@
         @pl.when(self.follow)
         def _():
             for c in ORDER:
-                for which in range(2):
-                    self.share(c, which, which).wait_recv()
+                self.share(c, 1, 1).wait_recv()
 
     def finish(self):
         @pl.when(self.ends)
@@ -472,13 +478,15 @@
     spread.serve(5)
     spread.serve(6)
     spread.serve(7)
+    spread.half_end()
+    early = spread.early
+    vec_high[1 + early], vec_low[1 + early] = split(vec_row[early])
+    col_part(early)
     spread.end()
     row_scatter = ring_scatter(copies, row_sum, row_unit, row_relay, *z_ring, row_half, row_partner, pair_in.at[0])
     next(row_scatter)
-    vec_high[1], vec_low[1] = split(vec_row[0])
-    col_part(0)
-    vec_high[2], vec_low[2] = split(vec_row[1])
-    col_part(1)
+    vec_high[2 - early], vec_low[2 - early] = split(vec_row[1 - early])
+    col_part(1 - early)
     col_high[...], col_low[...] = split(parts[0])
     parts[0, rest_rows, :] += rest_part[...]
     columns = ring_scatter(copies, parts.at[0], col_unit, col_relay, *x_ring, lo, col_partner, pair_in.at[1])
@@ -558,9 +566,9 @@
     w_ref[...] = w
     w_high[0], w_low[0] = split(w)
     next(rows_in)
+    w_high[1 + core], w_low[1 + core] = split(av_row[core] - vec_middle[1 + core])
     step_all([rows_in])
-    for position in range(2):
-        w_high[1 + position], w_low[1 + position] = split(av_row[position] - vec_middle[1 + position])
+    w_high[2 - core], w_low[2 - core] = split(av_row[1 - core] - vec_middle[2 - core])
     copies.finish()
     spread.finish()
 

time: 81.2 us -> 81.6 us (level)
  no operation moved by 1% of the time
where the time goes in v9:
time: 81.6 us; the launch traced here: 81.5 us
  Pallas kernels  80.7 us (99%)
    pallas_call x1, Pallas kernels, shards(): pl.pallas_call(gather_kernel, out_shape=[terms, terms, terms, terms, jax....  73.7 us
    pallas_call x1, Pallas kernels, shards(): pl.pallas_call(update_kernel, out_shape=[jax.ShapeDtypeStruct(halves.shap...  6.94 us

profile of v9, /device:TPU:1, one launch (start us, length us, event | category | flops | bytes accessed | tf_op | source)
XLA Modules:
  0.0 81.5 jit_solution(1162746571280559458)
XLA Ops:
  0.6 0.0 copy-start
  0.6 73.7 %gather.1 = (bf16[3,1024,256]{2,1,0:T(8,128)(2,1)S(1)}, bf16[3,1024,256]{2,1,0:T(8,128)(2,1)S(1)}, bf16[3,1024,256]{2,1,0:T(8,128)(2,1)S(1)}, bf16[3,1024,256]{2,1,0:T(8,128)(2,1)S(1)}, f32[1024,256]{1,0:T(8,128)S(1)}) custom-call(f32[2,512,1024]{2,1,0:T(8,128)} %halves_ref.3, f32[64,1024]{1,0:T(8,128)} %rest_ref.1, f32[1024,256]{1,0:T(8,128)} %vec_hbm.1, ...), custom_call_target="tpu_custom_call" | custom-call | tf_op jit(solution)/shard_map/gather/pallas_call | solution.py:642
  74.4 0.0 copy-done
  74.4 6.9 %update.1 = (f32[2,512,1024]{2,1,0:T(8,128)}, f32[64,1024]{1,0:T(8,128)}, f32[1024,256]{1,0:T(8,128)}) custom-call(f32[2,512,1024]{2,1,0:T(8,128)S(1)} %copy-done, f32[64,1024]{1,0:T(8,128)} %rest_ref.1, bf16[3,1024,256]{2,1,0:T(8,128)(2,1)S(1)} %get-tuple-element.8.vec_high, bf16[3,1024,256]{2,1,0:T(8,128)(2,1)S(1)} %get-tuple-element.9.vec_low, ...), custom_call_target="tpu_custom_call" | custom-call | tf_op jit(solution)/shard_map/update/pallas_call | solution.py:692
Async XLA Ops:
  0.6 73.7 %copy-start = (f32[2,512,1024]{2,1,0:T(8,128)S(1)}, f32[2,512,1024]{2,1,0:T(8,128)}, u32[]{:S(2)}) copy-start(f32[2,512,1024]{2,1,0:T(8,128)} %halves_ref.3) | copy-start | bytes 12582916

commit v10 on v9

--- a/solution.py
+++ b/solution.py
@@ -620,7 +620,7 @@
         store(at_step).start()
         return carry
 
-    lax.fori_loop(0, count, one, 0)
+    lax.fori_loop(0, count, one, 0, unroll=True)
     for at_step in range(count):
         store(at_step).wait()
     w_copy.wait()

time: 81.6 us -> 80.5 us (0.987)
  Pallas kernels: 80.7 us -> 79.6 us
    pallas_call x1, Pallas kernels: 6.94 us -> 5.85 us  [shards(): pl.pallas_call(update_kernel, out_shape=[jax.ShapeDtypeStruct(halves.shap...]
where the time goes in v10:
time: 80.5 us; the launch traced here: 80.4 us
  Pallas kernels  79.6 us (99%)
  between operations  0.81 us (1%)
    pallas_call x1, Pallas kernels, shards(): pl.pallas_call(gather_kernel, out_shape=[terms, terms, terms, terms, jax....  73.7 us
    pallas_call x1, Pallas kernels, shards(): pl.pallas_call(update_kernel, out_shape=[jax.ShapeDtypeStruct(halves.shap...  5.85 us

profile of v10, /device:TPU:1, one launch (start us, length us, event | category | flops | bytes accessed | tf_op | source)
XLA Modules:
  0.0 80.4 jit_solution(7563951695003670689)
XLA Ops:
  0.6 0.0 copy-start
  0.6 73.7 %gather.1 = (bf16[3,1024,256]{2,1,0:T(8,128)(2,1)S(1)}, bf16[3,1024,256]{2,1,0:T(8,128)(2,1)S(1)}, bf16[3,1024,256]{2,1,0:T(8,128)(2,1)S(1)}, bf16[3,1024,256]{2,1,0:T(8,128)(2,1)S(1)}, f32[1024,256]{1,0:T(8,128)S(1)}) custom-call(f32[2,512,1024]{2,1,0:T(8,128)} %halves_ref.3, f32[64,1024]{1,0:T(8,128)} %rest_ref.1, f32[1024,256]{1,0:T(8,128)} %vec_hbm.1, ...), custom_call_target="tpu_custom_call" | custom-call | tf_op jit(solution)/shard_map/gather/pallas_call | solution.py:642
  74.4 0.0 copy-done
  74.4 5.9 %update.1 = (f32[2,512,1024]{2,1,0:T(8,128)}, f32[64,1024]{1,0:T(8,128)}, f32[1024,256]{1,0:T(8,128)}) custom-call(f32[2,512,1024]{2,1,0:T(8,128)S(1)} %copy-done, f32[64,1024]{1,0:T(8,128)} %rest_ref.1, bf16[3,1024,256]{2,1,0:T(8,128)(2,1)S(1)} %get-tuple-element.8.vec_high, bf16[3,1024,256]{2,1,0:T(8,128)(2,1)S(1)} %get-tuple-element.9.vec_low, ...), custom_call_target="tpu_custom_call" | custom-call | tf_op jit(solution)/shard_map/update/pallas_call | solution.py:692
Async XLA Ops:
  0.6 73.7 %copy-start = (f32[2,512,1024]{2,1,0:T(8,128)S(1)}, f32[2,512,1024]{2,1,0:T(8,128)}, u32[]{:S(2)}) copy-start(f32[2,512,1024]{2,1,0:T(8,128)} %halves_ref.3) | copy-start | bytes 12582916
